TPU v7x, 32 devices: a whole 2x2x4 slice. The times are simulated.
32 devices in a mesh: tm: 8 (over z, x), chan: 4 (over y, core).
Axes of the slice: x: 2, y: 2, z: 4, core: 2. Of those that a mesh axis runs over, the one named last changes fastest.
Arguments:
- data: bfloat16 [1024, 10240], P('chan', 'tm'), may hold values from -80 to 80
- templates: bfloat16 [1024, 102400], P('tm', 'chan'), may hold values from -6 to 6
- valid: int32 [1024, 1024], P('tm', 'chan'), may hold values from 0 to 1, as said below
Outputs:
- detection: float32 [3, 128, 10240], P(None, 'chan', 'tm')
Inputs may be any that keep to these rules, and one draw needn't show every extreme that they name: `valid`: template number r uses channel r mod 1024.
All inputs are finite; a program needn't handle non-finite values.
Results may differ from a plain program's by a relative error of at most 0.0003.
Values may be sent and summed in bfloat16 or wider, within the bound.
No kernel may reach another device: no remote copies, remote signals or barrier semaphores. Data moves between devices by JAX's collectives and lax.ppermute only.
A program may use at most 128 MiB of HBM per device.

v0:
```python
import jax
import jax.numpy as jnp
from jax import lax
from jax.sharding import PartitionSpec as P

TLEN = 100


EPSILON = 1e-06


def shifted(block, axis, distance):
    devices = range(lax.axis_size(axis))
    route = [(i - distance, i) for i in devices if i - distance in devices]
    return lax.ppermute(block, axis, route)


def passed_along(block, axis, distance):
    devices = range(lax.axis_size(axis))
    route = [((i - distance) % len(devices), i) for i in devices]
    return lax.ppermute(block, axis, route)


def window_energy(segment):
    squares = jnp.square(segment.astype(jnp.float32))
    return lax.reduce_window(squares, jnp.float32(0.0), lax.add, (1, TLEN), (1, 1), "VALID")


def block_terms(segment, energy, block, weights):
    rows = block.shape[0]
    chans = weights.shape[1]
    kernel = block.reshape(rows, chans, TLEN) * weights[:, :, None]
    num = lax.conv_general_dilated(
        segment[None],
        kernel,
        (1,),
        "VALID",
        dimension_numbers=("NCH", "OIH", "NCH"),
        preferred_element_type=jnp.float32,
    )[0]
    weights_wide = weights.astype(jnp.float32)
    esum = jnp.dot(weights_wide, energy, precision=lax.Precision.HIGHEST)
    tnorm = jnp.sum(jnp.square(kernel.astype(jnp.float32)), axis=(1, 2))
    count = jnp.sum(weights_wide, axis=1)
    return (num, esum, tnorm, count)


def finish(num, esum, tnorm, count):
    scale = jnp.sqrt(count * TLEN)
    return num * scale[..., None] * lax.rsqrt(esum * tnorm[..., None] + EPSILON)


def local(data, templates, valid):
    tail = shifted(data[:, : TLEN - 1], "tm", -1)
    segment = jnp.concatenate([data, tail], axis=1)
    energy = window_energy(segment)
    weights = valid.astype(jnp.bfloat16)
    earlier = passed_along(segment, "tm", 1)
    earliest = passed_along(earlier, "tm", 1)
    pieces = [
        block_terms(segment, energy, templates, weights),
        block_terms(earlier, window_energy(earlier), templates, weights),
        block_terms(earliest, window_energy(earliest), templates, weights),
    ]
    stacked = [jnp.stack([piece[number] for piece in pieces]) for number in range(4)]
    summed = (
        lax.psum_scatter(stacked[0], "chan", scatter_dimension=1, tiled=True),
        lax.psum_scatter(stacked[1], "chan", scatter_dimension=1, tiled=True),
        lax.psum_scatter(stacked[2], "chan", scatter_dimension=1, tiled=True),
        lax.psum_scatter(stacked[3], "chan", scatter_dimension=1, tiled=True),
    )
    traces = finish(summed[0], summed[1], summed[2], summed[3])
    home_one = passed_along(traces[1], "tm", -1)
    home_two = passed_along(traces[2], "tm", -2)
    traces = jnp.stack([traces[0], home_one, home_two])
    return traces


def solution(mesh):
    placed = (P("chan", "tm"), P("tm", "chan"), P("tm", "chan"))
    return jax.shard_map(
        local, mesh=mesh, in_specs=placed, out_specs=P(None, "chan", "tm"), check_vma=False
    )
```

profile of v0, /device:TPU:0, one launch (start us, length us, event | category | flops | bytes accessed | tf_op | source)
XLA Modules:
  0.0 413.6 jit_solution(6701027908526966731)
XLA Ops:
  11.1 3.7 mul.46.clone
  14.8 9.8 %mul.52 = bf16[128,25600]{0,1:T(8,128)(2,1)} reshape(bf16[128,256,100]{0,2,1:T(8,128)(2,1)} %mul.46.clone) | data formatting | bytes 13107200 | tf_op jit(solution)/shard_map/mul | solution.py:32
  24.6 9.8 %copy.71 = bf16[128,25600]{0,1:T(8,128)(2,1)} copy(bf16[128,25600]{1,0:T(8,128)(2,1)} %param.4) | data formatting | bytes 13107200 | tf_op args[1]
  34.4 6.8 %multiply_reduce_fusion = f32[128]{0:T(128)S(1)} fusion(bf16[128,25600]{0,1:T(8,128)(2,1)} %copy.71, bf16[128,25600]{0,1:T(8,128)(2,1)} %mul.52), kind=kLoop, calls=%fused_computation | loop fusion | flops 13107072 | bytes 13107712 | tf_op jit(solution)/shard_map/reduce_sum | solution.py:43
  41.9 33.9 %reshape.50 = bf16[128,256,100]{2,1,0:T(8,128)(2,1)} reshape(bf16[128,25600]{1,0:T(8,128)(2,1)} %param.4) | data formatting | bytes 13107200 | tf_op jit(solution)/shard_map/reshape | solution.py:32
  75.8 11.7 %copy.59 = bf16[128,256,100]{1,0,2:T(8,128)(2,1)} copy(bf16[128,256,100]{2,1,0:T(8,128)(2,1)} %reshape.50) | data formatting | bytes 13107200 | tf_op jit(solution)/shard_map/reshape | solution.py:32
  88.6 3.7 collective-permute-start.1
  93.1 22.4 %fusion.12 = f32[8,173,128]{2,0,1:T(8,128)S(1)} fusion(bf16[128,256,100]{1,0,2:T(8,128)(2,1)} %copy.59, bf16[128,256]{1,0:T(8,128)(2,1)S(1)} %get-tuple-element.8, bf16[256,1,7,99]{0,2,3,1:T(8,128)(2,1)S(1)} %slice.23, bf16[256,1,8,173]{0,2,3,1:T(8,128)(2,1)S(1)} %copy.57, pred[8,173]{0,1:T(8,128)(4,1)S(1)} %copy-done.6), kind=kOutput, calls=%fused_computation.22 | convolution fusion | flops 9076978688 | bytes 8392552 | tf_op jit(solution)/shard_map/conv_general_dilated | solution.py:33
  116.6 34.8 %reduce_window.21 = f32[256,1280]{0,1:T(8,128)S(1)} reduce-window(f32[256,1379]{0,1:T(8,128)S(1)} %convert_multiply_fusion.2, f32[]{:T(128)} %constant.0.clone.1), window={size=1x100}, to_apply=%region_3.0 | reduce-window | flops 32440320 | bytes 2722820 | tf_op jit(solution)/shard_map/reduce_window | solution.py:26
  151.5 1.6 convolution_bitcast_fusion.2
  155.7 3.4 collective-permute-start.2
  159.0 22.4 %fusion.15 = f32[8,173,128]{2,0,1:T(8,128)S(1)} fusion(bf16[128,256,100]{1,0,2:T(8,128)(2,1)} %copy.59, bf16[128,256]{1,0:T(8,128)(2,1)S(1)} %get-tuple-element.8, bf16[256,1,7,99]{0,2,3,1:T(8,128)(2,1)S(1)} %slice.25, bf16[256,1,8,173]{0,2,3,1:T(8,128)(2,1)S(1)} %copy.62, pred[8,173]{0,1:T(8,128)(4,1)S(1)} %copy-done.6), kind=kOutput, calls=%fused_computation.23 | convolution fusion | flops 9076978688 | bytes 8392552 | tf_op jit(solution)/shard_map/conv_general_dilated | solution.py:33
  183.7 34.9 %reduce_window.22 = f32[256,1280]{0,1:T(8,128)S(1)} reduce-window(f32[256,1379]{0,1:T(8,128)S(1)} %convert_multiply_fusion.1, f32[]{:T(128)} %constant.0.clone.1), window={size=1x100}, to_apply=%region_4.0 | reduce-window | flops 32440320 | bytes 2722820 | tf_op jit(solution)/shard_map/reduce_window | solution.py:26
  218.5 1.6 convolution_bitcast_fusion.1
  220.7 22.8 %fusion.18 = f32[8,173,128]{2,0,1:T(8,128)S(1)} fusion(bf16[128,256,100]{1,0,2:T(8,128)(2,1)} %copy.59, bf16[128,256]{1,0:T(8,128)(2,1)S(1)} %get-tuple-element.8, bf16[256,1,7,99]{0,2,3,1:T(8,128)(2,1)S(1)} %slice.27, bf16[256,1,8,173]{0,2,3,1:T(8,128)(2,1)S(1)} %copy.65, pred[8,173]{0,1:T(8,128)(4,1)S(1)} %copy-done.6), kind=kOutput, calls=%fused_computation.24 | convolution fusion | flops 9076978688 | bytes 8392552 | tf_op jit(solution)/shard_map/conv_general_dilated | solution.py:33
  244.7 34.7 %reduce_window.23 = f32[256,1280]{0,1:T(8,128)S(1)} reduce-window(f32[256,1379]{0,1:T(8,128)S(1)} %convert_multiply_fusion, f32[]{:T(128)} %constant.0.clone.1), window={size=1x100}, to_apply=%region_5.0 | reduce-window | flops 32440320 | bytes 2722820 | tf_op jit(solution)/shard_map/reduce_window | solution.py:26
  282.0 1.4 pad_maximum_fusion.1
  283.4 3.0 copy.67
  286.4 4.1 copy.69
  293.2 99.6 %all-reduce.5.cloned.1.call-done = (f32[3,128,1280]{2,0,1:T(4,128)}, f32[3,128,1280]{2,0,1:T(4,128)}) async-done(((f32[3,128,1280]{2,0,1:T(4,128)}, f32[3,128,1280]{2,0,1:T(4,128)}), (f32[3,128,1280]{2,0,1:T(4,128)}, f32[3,128,1280]{2,0,1:T(4,128)})) %all-reduce.5.cloned.1.call-update) | async-done | bytes 3932176
  392.8 1.6 fusion.41
  394.8 4.3 %collective-permute-start.3 = (f32[32,1280]{1,0:T(8,128)S(1)}, f32[32,1280]{1,0:T(8,128)S(1)}, u32[]{:S(2)}, u32[]{:S(2)}) collective-permute-start(f32[32,1280]{1,0:T(8,128)S(1)} %bitcast.59), channel_id=1, source_target_pairs={{4,0},{8,4},{12,8},{16,12},{20,16},{24,20},{28,24},{0,28},{5,1},{9... | collective-permute-start | bytes 491528 | tf_op jit(solution)/shard_map/ppermute | solution.py:21
  399.7 4.0 collective-permute-done.3
  403.7 2.2 collective-permute-done.4
  (70 shorter events, 21.2 us)
Async XLA Ops:
  6.5 285.8 %reduce-scatter.7.cloned.1.call-start = ((), (), s32[]{:S(2)}) async-start(), calls=%async_computation.2 | async-start | bytes 81920
  7.9 79.7 %collective-permute-start = (bf16[256,99]{0,1:T(8,128)(2,1)S(1)}, bf16[256,99]{0,1:T(8,128)(2,1)S(1)}, u32[]{:S(2)}, u32[]{:S(2)}) collective-permute-start(bf16[256,99]{0,1:T(8,128)(2,1)S(1)} %slice.22), channel_id=1, source_target_pairs={{4,0},{8,4},{12,8},{16,12},{20,16},{24,20},{28,24},{5,1},{9,5},{13... | collective-permute-start | bytes 152072 | tf_op jit(solution)/shard_map/ppermute | solution.py:15
  10.9 282.3 %reduce-scatter.9.cloned.1.call-start = ((), (), s32[]{:S(2)}) async-start(), calls=%async_computation.3 | async-start | bytes 81920
  41.9 350.9 %all-reduce.5.cloned.1.call-start = ((), (), s32[]{:S(2)}) async-start(), calls=%async_computation.4 | async-start | bytes 10485760
  88.6 65.4 %collective-permute-start.1 = (bf16[256,1379]{0,1:T(8,128)(2,1)}, bf16[256,1379]{0,1:T(8,128)(2,1)}, u32[]{:S(2)}, u32[]{:S(2)}) collective-permute-start(bf16[256,1379]{0,1:T(8,128)(2,1)} %get-tuple-element.10), channel_id=1, source_target_pairs={{28,0},{0,4},{4,8},{8,12},{12,16},{16,20},{20,24},{24,28},{29,1},{... | collective-permute-start | bytes 2118152 | tf_op jit(solution)/shard_map/ppermute | solution.py:21
  92.3 0.7 copy-start.6
  151.5 1.6 copy-start.2
  155.7 64.4 %collective-permute-start.2 = (bf16[256,1379]{0,1:T(8,128)(2,1)}, bf16[256,1379]{0,1:T(8,128)(2,1)S(1)}, u32[]{:S(2)}, u32[]{:S(2)}) collective-permute-start(bf16[256,1379]{0,1:T(8,128)(2,1)} %collective-permute-done.1), channel_id=1, source_target_pairs={{28,0},{0,4},{4,8},{8,12},{12,16},{16,20},{20,24},{24,28},{29,1},{... | collective-permute-start | bytes 2118152 | tf_op jit(solution)/shard_map/ppermute | solution.py:21
  244.7 35.5 %copy-start = (f32[1,1384,128]{2,1,0:T(8,128)S(1)}, f32[1,1384,128]{2,1,0:T(8,128)}, u32[]{:S(2)}) copy-start(f32[1,1384,128]{2,1,0:T(8,128)} %reshape.27) | copy-start | bytes 2125828
  279.4 1.1 copy-start.1
  279.4 1.3 copy-start.4
  280.7 1.1 copy-start.3
  280.7 1.3 copy-start.5
  290.5 0.7 copy-start.7
  394.8 8.9 %collective-permute-start.3 = (f32[32,1280]{1,0:T(8,128)S(1)}, f32[32,1280]{1,0:T(8,128)S(1)}, u32[]{:S(2)}, u32[]{:S(2)}) collective-permute-start(f32[32,1280]{1,0:T(8,128)S(1)} %bitcast.59), channel_id=1, source_target_pairs={{4,0},{8,4},{12,8},{16,12},{20,16},{24,20},{28,24},{0,28},{5,1},{9... | collective-permute-start | bytes 491528 | tf_op jit(solution)/shard_map/ppermute | solution.py:21
  399.1 6.8 %collective-permute-start.4 = (f32[32,1280]{1,0:T(8,128)S(1)}, f32[32,1280]{1,0:T(8,128)S(1)}, u32[]{:S(2)}, u32[]{:S(2)}) collective-permute-start(f32[32,1280]{1,0:T(8,128)S(1)} %bitcast.60), channel_id=1, source_target_pairs={{8,0},{12,4},{16,8},{20,12},{24,16},{28,20},{0,24},{4,28},{9,1},{1... | collective-permute-start | bytes 491528 | tf_op jit(solution)/shard_map/ppermute | solution.py:21
Sparse Core Ops, SparseCore 0:
  11.1 23.2 reduce-scatter.6
  42.0 23.2 reduce-scatter.8
  290.6 102.0 all-reduce.4
where the time goes:
time: 420 us; the launch traced here: 414 us
  other arithmetic  119 us (28%)
  waiting for transfers between devices  106 us (25%)
  local copies, waits for them, and re-layouts  90 us (21%)
  matrix products  71.5 us (17%)
  between operations  14.4 us (3%)
  starting transfers between devices  13.3 us (3%)
    another operation x3, other arithmetic, window_energy(): lax.reduce_window(squares, jnp.float32(0.0), lax.add, (1, TLEN), (1, 1),...  104 us
    unnamed x6, waiting for transfers between devices  99.6 us
    conv_general_dilated x3, matrix products, block_terms(): lax.conv_general_dilated(segment[None], kernel, (1,), 'VALID', dimension_...  67.6 us
    reshape x2, local copies, waits for them, and re-layouts, block_terms(): kernel = block.reshape(rows, chans, TLEN) * weights[:, :, None]  45.6 us
    unnamed x25, local copies, waits for them, and re-layouts  16.4 us
    mul x2, local copies, waits for them, and re-layouts, block_terms(): kernel = block.reshape(rows, chans, TLEN) * weights[:, :, None]  13.5 us
    ppermute x4, starting transfers between devices, passed_along(): return lax.ppermute(block, axis, route)  12 us
  transfers between devices with their start and end apart: 8, of which 3 were waited for; matrix products, arithmetic and copies ran while one was open for 66% of the time, Pallas kernels for 0%

commit v1 on v0

v1 whole, which is shorter than its diff:
```python
import jax, jax.numpy as jnp
from jax import lax
from jax.experimental import pallas as pl
from jax.experimental.pallas import tpu as pltpu
from jax.sharding import PartitionSpec as P

TLEN = 100
EPSILON = 1e-06
SIDE = 16
STEP = 32
EDGE = 128
LIMIT = 56 * 1024 * 1024
PAIRS = (TLEN + 2) // 2
TAPS = 2 * PAIRS + 1
Q = 17

VMEM = pl.BlockSpec(memory_space=pltpu.VMEM)
SMEM = pl.BlockSpec(memory_space=pltpu.SMEM)
ANY = pl.BlockSpec(memory_space=pl.ANY)


def relayout(t_hbm, v_ref, w, t_all, tall, mask, arrived):
    chans = v_ref.shape[1]
    steps = chans // STEP
    wide = STEP * TLEN
    mask[...] = v_ref[...].astype(jnp.float32).T
    blank = jnp.zeros(w.shape[1:], w.dtype)
    w[0] = blank
    for tap in range(TLEN + 1, TAPS):
        w[tap] = blank

    def step(i, total):
        columns = pl.ds(pl.multiple_of(i * wide, wide), wide)
        channels = pl.ds(pl.multiple_of(i * STEP, STEP), STEP)
        pltpu.make_async_copy(t_hbm.at[:, columns], t_all.at[:, columns], arrived.at[i]).wait()
        tall[...] = t_all[:, columns].T.astype(jnp.float32)
        keep = mask[channels, :]

        def tap(l, total):
            kernel = tall[pl.ds(l, STEP, stride=TLEN), :] * keep
            w[l + 1, channels, :] = kernel.astype(w.dtype)
            return total + kernel * kernel

        return lax.fori_loop(0, TLEN, tap, total, unroll=10)

    total = lax.fori_loop(0, steps, step, jnp.zeros((STEP, w.shape[2]), jnp.float32))
    norm = jnp.sum(total, axis=0, keepdims=True)
    return jnp.broadcast_to(norm, (128, norm.shape[1])).T


def interleave(x_ref, h_ref, turned, windows):
    chans, slab = x_ref.shape
    lanes = turned.shape[2]
    reach = windows.shape[0] // SIDE
    step = slab // SIDE
    for b in range(turned.shape[0]):
        rows = slice(b * lanes, min((b + 1) * lanes, chans))
        n = rows.stop - rows.start
        turned[b, :slab, :n] = x_ref[rows, :].T.astype(jnp.float32)
        turned[b, slab:, :n] = h_ref[rows, :].T.astype(jnp.float32)
    for a in range(reach):
        for p in range(2):
            for b in range(turned.shape[0]):
                n = min(lanes, chans - b * lanes)
                samples = turned[b, pl.ds(2 * a + p, SIDE, stride=step), :]
                at = p * chans + b * lanes
                windows[a * SIDE:(a + 1) * SIDE, at:at + n] = samples[:, :n].astype(windows.dtype)


def correlate(w, windows, acc, flat, before):
    half, rows = acc.shape[1:]
    acc[...] = jnp.zeros_like(acc)

    def group(g, carry):
        before(g)
        left, right = [], []
        for k in range(Q):
            q = g * Q + k
            left.append(windows[pl.ds(pl.multiple_of(q * SIDE, SIDE), half), :])
            for m in (2 * q, 2 * q + 1):
                right.append(jnp.concatenate([w[m + 1], w[m]], axis=1))
        d = jnp.dot(jnp.concatenate(left, axis=1), jnp.concatenate(right, axis=0), preferred_element_type=jnp.float32)
        for r in range(2):
            acc[r] += d[:, r * rows:(r + 1) * rows]
        return carry

    lax.fori_loop(0, PAIRS // Q, group, 0)
    inner = half // SIDE
    step = 2 * inner
    for r in range(2):
        for b in range(SIDE):
            flat[pl.ds(step * b + r, inner, stride=2), :] = acc[r, pl.ds(b, inner, stride=SIDE), :]


def split(whole, mine, keep_ref, give_ref):
    pieces, piece = keep_ref.shape[:2]
    for i in range(pieces):
        at = pl.multiple_of((2 * i + mine) * piece, piece)
        keep_ref[i] = whole[pl.ds(at, piece), :]
        at = pl.multiple_of((2 * i + 1 - mine) * piece, piece)
        give_ref[i] = whole[pl.ds(at, piece), :]


def first_kernel(bit_ref, t_hbm, v_ref, v1_ref, v2_ref, x_ref, h_ref,
                 w_hbm, keep_ref, give_ref, skeep_ref, sgive_ref,
                 w, t_all, tall, mask, turned, windows, acc, flat, whole, power, arrived, left):
    chans, slab = x_ref.shape
    wide = STEP * TLEN
    for i in range(chans // STEP):
        columns = pl.ds(i * wide, wide)
        pltpu.make_async_copy(t_hbm.at[:, columns], t_all.at[:, columns], arrived.at[i]).start()
    interleave(x_ref, h_ref, turned, windows)
    norm = relayout(t_hbm, v_ref, w, t_all, tall, mask, arrived)
    out = pltpu.make_async_copy(w, w_hbm, left)
    out.start()
    mine = bit_ref[0]
    valids = [r[...].astype(jnp.bfloat16) for r in (v_ref, v1_ref, v2_ref)]
    for at in range(0, slab + EDGE, 128):
        part = x_ref[:, at:at + 128] if at < slab else h_ref[:, at - slab:at - slab + 128]
        square = jnp.square(part.astype(jnp.float32))
        high = square.astype(jnp.bfloat16)
        low = (square - high.astype(jnp.float32)).astype(jnp.bfloat16)
        for j in range(3):
            power[j, :, at:at + 128] = jnp.dot(valids[j], high, preferred_element_type=jnp.float32) + jnp.dot(valids[j], low, preferred_element_type=jnp.float32)
    for j in range(3):
        count = jnp.sum(valids[j].astype(jnp.float32), axis=1, keepdims=True)
        lane = lax.broadcasted_iota(jnp.int32, norm.shape, 1)
        power[j, :, slab + EDGE:] = jnp.where(lane < 64, count, norm)
    for j in range(3):
        split(power.at[j], mine, skeep_ref.at[j], sgive_ref.at[j])
    correlate(w, windows, acc, flat, lambda g: None)
    whole[...] = flat[...].T
    split(whole, mine, keep_ref, give_ref)
    out.wait()


def later_kernel(bit_ref, w_hbm, x_ref, next_hbm, keep_ref, give_ref, h_ref, w, turned, windows, acc, flat, whole, arrived):
    groups = PAIRS // Q

    def piece(g):
        lo = g * 2 * Q
        return pltpu.make_async_copy(w_hbm.at[pl.ds(lo, 2 * Q)], w.at[pl.ds(lo, 2 * Q)], arrived.at[g])

    for g in range(groups):
        piece(g).start()
    last = pltpu.make_async_copy(w_hbm.at[pl.ds(TAPS - 1, 1)], w.at[pl.ds(TAPS - 1, 1)], arrived.at[groups])
    last.start()
    edge = pltpu.make_async_copy(next_hbm.at[:, pl.ds(0, EDGE)], h_ref, arrived.at[groups + 1])
    edge.start()
    edge.wait()
    h_ref[...] = h_ref[...] * bit_ref[1].astype(jnp.bfloat16)
    interleave(x_ref, h_ref, turned, windows)
    last.wait()
    piece(0).wait()

    def before(g):
        @pl.when(g + 1 < groups)
        def _():
            piece(g + 1).wait()

    correlate(w, windows, acc, flat, before)
    whole[...] = flat[...].T
    split(whole, bit_ref[0], keep_ref, give_ref)


def sizes(chans, slab, rows):
    half = slab // 2
    lanes = 128
    blocks = -(-chans // lanes)
    reach = half // SIDE + PAIRS - 1
    return [
        pltpu.VMEM((blocks, slab + EDGE, lanes), jnp.float32),
        pltpu.VMEM((reach * SIDE, 2 * chans), jnp.bfloat16),
        pltpu.VMEM((2, half, rows), jnp.float32),
        pltpu.VMEM((slab, rows), jnp.float32),
        pltpu.VMEM((rows, slab), jnp.float32),
    ]


def first(bit, templates, valid, valid1, valid2, x, h, pieces):
    chans, slab = x.shape
    rows = templates.shape[0]
    piece = rows // pieces
    f32, bf16 = jnp.float32, jnp.bfloat16
    wide = slab + EDGE + 128
    return pl.pallas_call(
        first_kernel,
        in_specs=[SMEM, ANY] + [VMEM] * 5,
        out_specs=[ANY] + [VMEM] * 4,
        out_shape=[
            jax.ShapeDtypeStruct((TAPS, chans, rows), bf16),
            jax.ShapeDtypeStruct((pieces // 2, piece, slab), f32),
            jax.ShapeDtypeStruct((pieces // 2, piece, slab), f32),
            jax.ShapeDtypeStruct((3, pieces // 2, piece, wide), f32),
            jax.ShapeDtypeStruct((3, pieces // 2, piece, wide), f32),
        ],
        scratch_shapes=[
            pltpu.VMEM((TAPS, chans, rows), bf16),
            pltpu.VMEM((rows, chans * TLEN), bf16),
            pltpu.VMEM((STEP * TLEN, rows), f32),
            pltpu.VMEM((chans, rows), f32),
        ] + sizes(chans, slab, rows) + [
            pltpu.VMEM((3, rows, wide), f32),
            pltpu.SemaphoreType.DMA((chans // STEP,)),
            pltpu.SemaphoreType.DMA,
        ],
        compiler_params=pltpu.CompilerParams(vmem_limit_bytes=LIMIT),
        cost_estimate=pl.CostEstimate(flops=2 * rows * chans * TLEN * slab, bytes_accessed=4 * rows * chans * TLEN, transcendentals=0),
    )(bit, templates, valid, valid1, valid2, x, h)


def later(bit, w, x, follows, pieces):
    chans, slab = x.shape
    rows = w.shape[2]
    piece = rows // pieces
    f32 = jnp.float32
    return pl.pallas_call(
        later_kernel,
        in_specs=[SMEM, ANY, VMEM, ANY],
        out_specs=[VMEM] * 2,
        out_shape=[jax.ShapeDtypeStruct((pieces // 2, piece, slab), f32)] * 2,
        scratch_shapes=[pltpu.VMEM((chans, EDGE), x.dtype), pltpu.VMEM(w.shape, w.dtype)] + sizes(chans, slab, rows) + [pltpu.SemaphoreType.DMA((PAIRS // Q + 2,))],
        compiler_params=pltpu.CompilerParams(vmem_limit_bytes=LIMIT),
        cost_estimate=pl.CostEstimate(flops=2 * rows * chans * TLEN * slab, bytes_accessed=2 * rows * chans * TLEN, transcendentals=0),
    )(bit, w, x, follows)


def window_kernel(p_ref, esum_ref):
    slab = esum_ref.shape[2]
    wide = slab + EDGE
    for j in range(p_ref.shape[0]):
        sums = {1: p_ref[j, :, :wide]}
        for reach in (1, 2, 4, 8, 16, 32):
            sums[2 * reach] = sums[reach] + pltpu.roll(sums[reach], wide - reach, 1)
        total = sums[64] + pltpu.roll(sums[32], wide - 64, 1) + pltpu.roll(sums[4], wide - 96, 1)
        esum_ref[j] = total[:, :slab]


def window(power):
    blocks, piece, wide = power.shape
    return pl.pallas_call(
        window_kernel,
        in_specs=[VMEM],
        out_specs=VMEM,
        out_shape=jax.ShapeDtypeStruct((blocks, piece, wide - EDGE - 128), jnp.float32),
    )(power)


def finish_kernel(esum_ref, c_ref, n0_ref, n1_ref, n2_ref, out_ref):
    slab = out_ref.shape[2]
    for j, n_ref in enumerate((n0_ref, n1_ref, n2_ref)):
        count = c_ref[j, :, :1]
        norm = n_ref[:, slab + 64:slab + 65]
        scale = jnp.sqrt(count * TLEN)
        out_ref[j] = n_ref[:, :slab] * scale * lax.rsqrt(esum_ref[j] * norm + EPSILON)


def finish(esum, counts, n0, n1, n2):
    return pl.pallas_call(
        finish_kernel,
        in_specs=[VMEM] * 5,
        out_specs=VMEM,
        out_shape=jax.ShapeDtypeStruct(esum.shape, jnp.float32),
    )(esum, counts, n0, n1, n2)


def moved(block, distance):
    n = lax.axis_size("tm")
    return lax.ppermute(block, "tm", [(i, (i + distance) % n) for i in range(n)])


def swapped(block, distance):
    n = lax.axis_size("chan")
    return lax.ppermute(block, "chan", [(i, i ^ distance) for i in range(n)])


def scattered(keep, give, axis):
    distance = 1
    while True:
        total = keep + swapped(give, distance)
        left = total.shape[axis]
        if left == 1:
            return lax.squeeze(total, (axis,))
        distance *= 2
        mine = (lax.axis_index("chan") // distance) % 2
        shape = total.shape
        total = total.reshape(shape[:axis] + (left // 2, 2) + shape[axis + 1:])
        keep = lax.dynamic_index_in_dim(total, mine, axis + 1, keepdims=False)
        give = lax.dynamic_index_in_dim(total, 1 - mine, axis + 1, keepdims=False)


def local(data, templates, valid):
    pieces = lax.axis_size("chan")
    n = lax.axis_size("tm")
    at = lax.axis_index("tm")
    head = lax.ppermute(data[:, :EDGE], "tm", [(i + 1, i) for i in range(n - 1)])
    marks = valid.astype(jnp.bfloat16)
    marks1 = moved(marks, -1)
    marks2 = moved(marks, -2)
    earlier = moved(data, 1)
    earliest = moved(data, 2)
    mine = lax.axis_index("chan") % 2
    flags1 = jnp.stack([mine, (at != 0).astype(jnp.int32)])
    flags2 = jnp.stack([mine, (at != 1).astype(jnp.int32)])
    w, keep, give, power_keep, power_give = first(flags1, templates, marks, marks1, marks2, data, head, pieces)
    power = scattered(power_keep, power_give, 1)
    num0 = scattered(keep, give, 0)
    num1 = scattered(*later(flags1, w, earlier, data, pieces), 0)
    num2 = scattered(*later(flags2, w, earliest, earlier, pieces), 0)
    counts = power[:, :, -128:]
    norm = counts[0]
    home1 = moved(jnp.concatenate([num1, norm], axis=1), -1)
    home2 = moved(jnp.concatenate([num2, norm], axis=1), -2)
    return finish(window(power), counts, jnp.concatenate([num0, norm], axis=1), home1, home2)


def solution(mesh):
    placed = (P("chan", "tm"), P("tm", "chan"), P("tm", "chan"))
    return jax.shard_map(
        local, mesh=mesh, in_specs=placed, out_specs=P(None, "chan", "tm"), check_vma=False
    )
```

time: 420 us -> 122 us (0.29); the launches traced: 414 us -> 121 us
  other arithmetic: 119 us -> 3.34 us
  local copies, waits for them, and re-layouts: 90 us -> 6.28 us
  waiting for transfers between devices: 106 us -> 26.1 us
  matrix products: 71.5 us -> 0 us
  Pallas kernels: 0 us -> 56.6 us
  starting transfers between devices: 13.3 us -> 28.5 us
  between operations: 14.4 us -> 0.31 us
    another operation x6 -> x2, other arithmetic: 107 us -> 1.21 us  [the longest x1 0.65 us: local(): flags1 = jnp.stack([mine, (at != 0).astype(jnp.int32)])]
    unnamed x6 -> x0, waiting for transfers between devices: 99.6 us -> none
    conv_general_dilated x3 -> x0, matrix products: 67.6 us -> none  [block_terms(): lax.conv_general_dilated(segment[None], kernel, (1,), 'VALID', dimension_...]
    pallas_call x0 -> x5, Pallas kernels: none -> 56.6 us  [the longest x2 31.5 us: later(): pl.pallas_call(later_kernel, in_specs=[SMEM, ANY, VMEM, ANY], out_specs=[...]
    reshape x2 -> x0, local copies, waits for them, and re-layouts: 45.6 us -> none  [block_terms(): kernel = block.reshape(rows, chans, TLEN) * weights[:, :, None]]
    ppermute x5 -> x15, waiting for transfers between devices: 6.17 us -> 26.1 us  [the longest x8 19.3 us: swapped(): return lax.ppermute(block, 'chan', [(i, i ^ distance) for i in range(n)])]
    ppermute x5 -> x15, starting transfers between devices: 13.3 us -> 28.5 us  [the longest x6 21.7 us: moved(): lax.ppermute(block, 'tm', [(i, (i + distance) % n) for i in range(n)])]
    unnamed x25 -> x26, local copies, waits for them, and re-layouts: 16.4 us -> 2.43 us
  transfers between devices with their start and end apart: 8 -> 15, of which waited for: 3 -> 6; matrix products, arithmetic and copies ran while one was open for 66% -> 4% of each run, Pallas kernels for 0% -> 45%
where the time goes in v1:
time: 122 us; the launch traced here: 121 us
  Pallas kernels  56.6 us (46%)
  starting transfers between devices  28.5 us (23%)
  waiting for transfers between devices  26.1 us (21%)
  local copies, waits for them, and re-layouts  6.28 us (5%)
  other arithmetic  3.34 us (3%)
    pallas_call x2, Pallas kernels, later(): pl.pallas_call(later_kernel, in_specs=[SMEM, ANY, VMEM, ANY], out_specs=[...  31.5 us
    ppermute x6, starting transfers between devices, moved(): lax.ppermute(block, 'tm', [(i, (i + distance) % n) for i in range(n)])  21.7 us
    pallas_call x1, Pallas kernels, first(): pl.pallas_call(first_kernel, in_specs=[SMEM, ANY] + [VMEM] * 5, out_specs...  19.5 us
    ppermute x8, waiting for transfers between devices, swapped(): return lax.ppermute(block, 'chan', [(i, i ^ distance) for i in range(n)])  19.3 us
    ppermute x8, starting transfers between devices, swapped(): return lax.ppermute(block, 'chan', [(i, i ^ distance) for i in range(n)])  5.51 us
    ppermute x1, waiting for transfers between devices, local(): lax.ppermute(data[:, :EDGE], 'tm', [(i + 1, i) for i in range(n - 1)])  4.17 us
    pallas_call x1, Pallas kernels, window(): pl.pallas_call(window_kernel, in_specs=[VMEM], out_specs=VMEM, out_shape=...  3.41 us
    ppermute x6, waiting for transfers between devices, moved(): lax.ppermute(block, 'tm', [(i, (i + distance) % n) for i in range(n)])  2.68 us
  transfers between devices with their start and end apart: 15, of which 6 were waited for; matrix products, arithmetic and copies ran while one was open for 4% of the time, Pallas kernels for 45%

profile of v1, /device:TPU:0, one launch (start us, length us, event | category | flops | bytes accessed | tf_op | source)
XLA Modules:
  0.0 121.2 jit_solution(3870428498988593134)
XLA Ops:
  0.0 0.9 convert_element_type.2.v_ref
  0.9 6.0 %collective-permute-start = (bf16[128,256]{1,0:T(8,128)(2,1)S(1)}, bf16[128,256]{1,0:T(8,128)(2,1)S(1)}, u32[]{:S(2)}, u32[]{:S(2)}) collective-permute-start(bf16[128,256]{1,0:T(8,128)(2,1)S(1)} %convert_element_type.2.v_ref), channel_id=1, source_target_pairs={{0,28},{4,0},{8,4},{12,8},{16,12},{20,16},{24,20},{28,24},{1,29},{... | collective-permute-start | bytes 196616 | tf_op jit(solution)/shard_map/ppermute | solution.py:269
  7.4 1.6 %collective-permute-start.11 = (bf16[256,1280]{1,0:T(8,128)(2,1)}, bf16[256,1280]{1,0:T(8,128)(2,1)S(1)}, u32[]{:S(2)}, u32[]{:S(2)}) collective-permute-start(bf16[256,1280]{1,0:T(8,128)(2,1)} %next_hbm.1), channel_id=1, source_target_pairs={{0,8},{4,12},{8,16},{12,20},{16,24},{20,28},{24,0},{28,4},{1,9},{5... | collective-permute-start | bytes 1966088 | tf_op jit(solution)/shard_map/ppermute | solution.py:269
  9.0 0.9 slice.10
  9.9 1.3 %collective-permute-start.2 = (bf16[256,128]{1,0:T(8,128)(2,1)S(1)}, bf16[256,128]{1,0:T(8,128)(2,1)S(1)}, u32[]{:S(2)}, u32[]{:S(2)}) collective-permute-start(bf16[256,128]{1,0:T(8,128)(2,1)S(1)} %slice.10), channel_id=1, source_target_pairs={{4,0},{8,4},{12,8},{16,12},{20,16},{24,20},{28,24},{5,1},{9,5},{13... | collective-permute-start | bytes 196616 | tf_op jit(solution)/shard_map/ppermute | solution.py:296
  11.9 4.2 %collective-permute-done.2.h_ref = bf16[256,128]{1,0:T(8,128)(2,1)S(1)} collective-permute-done((bf16[256,128]{1,0:T(8,128)(2,1)S(1)}, bf16[256,128]{1,0:T(8,128)(2,1)S(1)}, u32[]{:S(2)}, u32[]{:S(2)}) %collective-permute-start.2) | collective-permute-done | bytes 65568 | tf_op jit(solution)/shard_map/ppermute | solution.py:296
  16.7 19.5 %shard_map.37 = (bf16[103,256,128]{2,1,0:T(8,128)(2,1)}, f32[2,32,1280]{2,1,0:T(8,128)}, f32[2,32,1280]{2,1,0:T(8,128)}, f32[3,2,32,1536]{3,2,1,0:T(8,128)}, f32[3,2,32,1536]{3,2,1,0:T(8,128)}) custom-call(s32[2]{0:T(128)} %pad_add_fusion.bit_ref, bf16[128,25600]{1,0:T(8,128)(2,1)} %t_hbm.1, bf16[128,256]{1,0:T(8,128)(2,1)} %copy-done.7, ...), custom_call_target="tpu_custom_call" | custom-call | flops 8388608000 | bytes 13107200 | tf_op jit(solution)/shard_map/pallas_call | solution.py:186
  36.9 1.4 %copy.4 = f32[3,2,32,1536]{3,2,0,1:T(8,128)S(1)} copy(f32[3,2,32,1536]{3,2,1,0:T(8,128)} %get-tuple-element.15) | data formatting | bytes 2359296 | tf_op jit(solution)/shard_map/pallas_call | solution.py:186
  38.9 1.6 %collective-permute-start.6 = (f32[1,32,1280]{2,1,0:T(8,128)S(1)}, f32[1,32,1280]{2,1,0:T(8,128)S(1)}, u32[]{:S(2)}, u32[]{:S(2)}) collective-permute-start(f32[1,32,1280]{2,1,0:T(8,128)S(1)} %constant_dynamic-slice_fusion.2), channel_id=1, source_target_pairs={{0,2},{1,3},{2,0},{3,1},{4,6},{5,7},{6,4},{7,5},{8,10},{9,11},{10,... | collective-permute-start | bytes 491528 | tf_op jit(solution)/shard_map/ppermute | solution.py:274
  40.5 0.9 copy-done.9
  41.6 15.6 %shard_map.40 = (f32[2,32,1280]{2,1,0:T(8,128)}, f32[2,32,1280]{2,1,0:T(8,128)}) custom-call(s32[2]{0:T(128)} %pad_add_fusion.1.bit_ref, bf16[103,256,128]{2,1,0:T(8,128)(2,1)} %get-tuple-element.18.w_hbm, bf16[256,1280]{1,0:T(8,128)(2,1)} %copy-done.9, bf16[256,1280]{1,0:T(8,128)(2,1)} %copy-done.8), custom_call_target="tpu_custom_call" | custom-call | flops 8388608000 | bytes 6553600 | tf_op jit(solution)/shard_map/pallas_call | solution.py:217
  57.3 15.9 %shard_map.39 = (f32[2,32,1280]{2,1,0:T(8,128)}, f32[2,32,1280]{2,1,0:T(8,128)}) custom-call(s32[2]{0:T(128)} %pad_add_fusion.bit_ref, bf16[103,256,128]{2,1,0:T(8,128)(2,1)} %get-tuple-element.18.w_hbm, bf16[256,1280]{1,0:T(8,128)(2,1)} %copy-done.8, bf16[256,1280]{1,0:T(8,128)(2,1)} %next_hbm.1), custom_call_target="tpu_custom_call" | custom-call | flops 8388608000 | bytes 6553600 | tf_op jit(solution)/shard_map/pallas_call | solution.py:217
  75.3 0.8 collective-permute-start.9
  76.3 1.3 %collective-permute-start.4 = (f32[3,1,32,1536]{3,2,0,1:T(8,128)S(1)}, f32[3,1,32,1536]{3,2,0,1:T(8,128)S(1)}, u32[]{:S(2)}, u32[]{:S(2)}) collective-permute-start(f32[3,1,32,1536]{3,2,0,1:T(8,128)S(1)} %constant_dynamic-slice_fusion.3), channel_id=1, source_target_pairs={{0,2},{1,3},{2,0},{3,1},{4,6},{5,7},{6,4},{7,5},{8,10},{9,11},{10,... | collective-permute-start | bytes 1769480 | tf_op jit(solution)/shard_map/ppermute | solution.py:274
  77.7 3.3 %collective-permute-done.13 = f32[1,32,1280]{2,1,0:T(8,128)S(1)} collective-permute-done((f32[1,32,1280]{2,1,0:T(8,128)S(1)}, f32[1,32,1280]{2,1,0:T(8,128)S(1)}, u32[]{:S(2)}, u32[]{:S(2)}) %collective-permute-start.13) | collective-permute-done | bytes 163872 | tf_op jit(solution)/shard_map/ppermute | solution.py:274
  81.0 3.5 %collective-permute-done.9 = f32[1,32,1280]{2,1,0:T(8,128)S(1)} collective-permute-done((f32[1,32,1280]{2,1,0:T(8,128)S(1)}, f32[1,32,1280]{2,1,0:T(8,128)S(1)}, u32[]{:S(2)}, u32[]{:S(2)}) %collective-permute-start.9) | collective-permute-done | bytes 163872 | tf_op jit(solution)/shard_map/ppermute | solution.py:274
  84.5 11.7 %collective-permute-done.4 = f32[3,1,32,1536]{3,2,0,1:T(8,128)S(1)} collective-permute-done((f32[3,1,32,1536]{3,2,0,1:T(8,128)S(1)}, f32[3,1,32,1536]{3,2,0,1:T(8,128)S(1)}, u32[]{:S(2)}, u32[]{:S(2)}) %collective-permute-start.4) | collective-permute-done | bytes 589856 | tf_op jit(solution)/shard_map/ppermute | solution.py:274
  96.3 0.8 pad_maximum_fusion
  97.1 2.0 %collective-permute-start.10 = (f32[32,1408]{1,0:T(8,128)S(1)}, f32[32,1408]{1,0:T(8,128)S(1)}, u32[]{:S(2)}, u32[]{:S(2)}) collective-permute-start(f32[32,1408]{1,0:T(8,128)S(1)} %get-tuple-element.24), channel_id=1, source_target_pairs={{0,28},{4,0},{8,4},{12,8},{16,12},{20,16},{24,20},{28,24},{1,29},{... | collective-permute-start | bytes 540680 | tf_op jit(solution)/shard_map/ppermute | solution.py:269
  99.1 11.7 %collective-permute-start.14 = (f32[32,1408]{1,0:T(8,128)S(1)}, f32[32,1408]{1,0:T(8,128)S(1)}, u32[]{:S(2)}, u32[]{:S(2)}) collective-permute-start(f32[32,1408]{1,0:T(8,128)S(1)} %get-tuple-element.23), channel_id=1, source_target_pairs={{0,24},{4,28},{8,0},{12,4},{16,8},{20,12},{24,16},{28,20},{1,25},{... | collective-permute-start | bytes 540680 | tf_op jit(solution)/shard_map/ppermute | solution.py:269
  110.8 3.4 %shard_map.38.esum_ref = f32[3,32,1280]{2,1,0:T(8,128)} custom-call(f32[3,32,1536]{2,1,0:T(8,128)} %copy-done), custom_call_target="tpu_custom_call" | custom-call | tf_op jit(solution)/shard_map/pallas_call | solution.py:241
  114.2 1.4 %slice.13.c_ref = f32[3,32,128]{2,1,0:T(8,128)} slice(f32[3,32,1536]{2,1,0:T(8,128)} %copy-done), slice={[0:3], [0:32], [1408:1536]} | slice | bytes 98304 | tf_op jit(solution)/shard_map/slice | solution.py:310
  115.7 2.7 %collective-permute-done.14.n2_ref = f32[32,1408]{1,0:T(8,128)S(1)} collective-permute-done((f32[32,1408]{1,0:T(8,128)S(1)}, f32[32,1408]{1,0:T(8,128)S(1)}, u32[]{:S(2)}, u32[]{:S(2)}) %collective-permute-start.14) | collective-permute-done | bytes 180256 | tf_op jit(solution)/shard_map/ppermute | solution.py:269
  119.0 2.2 %shard_map.41 = f32[3,32,1280]{2,1,0:T(8,128)} custom-call(f32[3,32,1280]{2,1,0:T(8,128)} %shard_map.38.esum_ref, f32[3,32,128]{2,1,0:T(8,128)} %slice.13.c_ref, f32[32,1408]{1,0:T(8,128)} %get-tuple-element.25.n0_ref, f32[32,1408]{1,0:T(8,128)} %copy-done.5, f32[32,1408]{1,0:T(8,128)} %copy-done.6), custom_call_target="tpu_custom_call" | custom-call | tf_op jit(solution)/shard_map/pallas_call | solution.py:259
  (57 shorter events, 6.3 us)
Async XLA Ops:
  0.9 15.1 %copy-start.7 = (bf16[128,256]{1,0:T(8,128)(2,1)}, bf16[128,256]{1,0:T(8,128)(2,1)S(1)}, u32[]{:S(2)}) copy-start(bf16[128,256]{1,0:T(8,128)(2,1)S(1)} %convert_element_type.2.v_ref) | copy-start | bytes 196612
  0.9 10.9 %collective-permute-start = (bf16[128,256]{1,0:T(8,128)(2,1)S(1)}, bf16[128,256]{1,0:T(8,128)(2,1)S(1)}, u32[]{:S(2)}, u32[]{:S(2)}) collective-permute-start(bf16[128,256]{1,0:T(8,128)(2,1)S(1)} %convert_element_type.2.v_ref), channel_id=1, source_target_pairs={{0,28},{4,0},{8,4},{12,8},{16,12},{20,16},{24,20},{28,24},{1,29},{... | collective-permute-start | bytes 196616 | tf_op jit(solution)/shard_map/ppermute | solution.py:269
  7.0 4.9 %collective-permute-start.1 = (bf16[128,256]{1,0:T(8,128)(2,1)S(1)}, bf16[128,256]{1,0:T(8,128)(2,1)S(1)}, u32[]{:S(2)}, u32[]{:S(2)}) collective-permute-start(bf16[128,256]{1,0:T(8,128)(2,1)S(1)} %convert_element_type.2.v_ref), channel_id=1, source_target_pairs={{0,24},{4,28},{8,0},{12,4},{16,8},{20,12},{24,16},{28,20},{1,25},{... | collective-permute-start | bytes 196616 | tf_op jit(solution)/shard_map/ppermute | solution.py:269
  7.4 33.1 %collective-permute-start.11 = (bf16[256,1280]{1,0:T(8,128)(2,1)}, bf16[256,1280]{1,0:T(8,128)(2,1)S(1)}, u32[]{:S(2)}, u32[]{:S(2)}) collective-permute-start(bf16[256,1280]{1,0:T(8,128)(2,1)} %next_hbm.1), channel_id=1, source_target_pairs={{0,8},{4,12},{8,16},{12,20},{16,24},{20,28},{24,0},{28,4},{1,9},{5... | collective-permute-start | bytes 1966088 | tf_op jit(solution)/shard_map/ppermute | solution.py:269
  9.0 31.5 %collective-permute-start.7 = (bf16[256,1280]{1,0:T(8,128)(2,1)}, bf16[256,1280]{1,0:T(8,128)(2,1)S(1)}, u32[]{:S(2)}, u32[]{:S(2)}) collective-permute-start(bf16[256,1280]{1,0:T(8,128)(2,1)} %next_hbm.1), channel_id=1, source_target_pairs={{0,4},{4,8},{8,12},{12,16},{16,20},{20,24},{24,28},{28,0},{1,5},{5... | collective-permute-start | bytes 1966088 | tf_op jit(solution)/shard_map/ppermute | solution.py:269
  9.9 6.1 %collective-permute-start.2 = (bf16[256,128]{1,0:T(8,128)(2,1)S(1)}, bf16[256,128]{1,0:T(8,128)(2,1)S(1)}, u32[]{:S(2)}, u32[]{:S(2)}) collective-permute-start(bf16[256,128]{1,0:T(8,128)(2,1)S(1)} %slice.10), channel_id=1, source_target_pairs={{4,0},{8,4},{12,8},{16,12},{20,16},{24,20},{28,24},{5,1},{9,5},{13... | collective-permute-start | bytes 196616 | tf_op jit(solution)/shard_map/ppermute | solution.py:296
  11.9 4.2 %copy-start.10 = (bf16[128,256]{1,0:T(8,128)(2,1)}, bf16[128,256]{1,0:T(8,128)(2,1)S(1)}, u32[]{:S(2)}) copy-start(bf16[128,256]{1,0:T(8,128)(2,1)S(1)} %collective-permute-done.v1_ref) | copy-start | bytes 196612
  11.9 4.2 %copy-start.11 = (bf16[128,256]{1,0:T(8,128)(2,1)}, bf16[128,256]{1,0:T(8,128)(2,1)S(1)}, u32[]{:S(2)}) copy-start(bf16[128,256]{1,0:T(8,128)(2,1)S(1)} %collective-permute-done.1.v2_ref) | copy-start | bytes 196612
  36.2 2.6 %collective-permute-start.5 = (f32[2,32,1280]{2,1,0:T(8,128)}, f32[2,32,1280]{2,1,0:T(8,128)S(1)}, u32[]{:S(2)}, u32[]{:S(2)}) collective-permute-start(f32[2,32,1280]{2,1,0:T(8,128)} %get-tuple-element.17), channel_id=1, source_target_pairs={{0,1},{1,0},{2,3},{3,2},{4,5},{5,4},{6,7},{7,6},{8,9},{9,8},{10,11... | collective-permute-start | bytes 983048 | tf_op jit(solution)/shard_map/ppermute | solution.py:274
  36.9 1.9 %copy-start.2 = (f32[2,32,1280]{2,1,0:T(8,128)S(1)}, f32[2,32,1280]{2,1,0:T(8,128)}, u32[]{:S(2)}) copy-start(f32[2,32,1280]{2,1,0:T(8,128)} %get-tuple-element.16) | copy-start | bytes 983044
  38.3 37.8 %collective-permute-start.3 = (f32[3,2,32,1536]{3,2,0,1:T(8,128)S(1)}, f32[3,2,32,1536]{3,2,0,1:T(8,128)S(1)}, u32[]{:S(2)}, u32[]{:S(2)}) collective-permute-start(f32[3,2,32,1536]{3,2,0,1:T(8,128)S(1)} %copy.4), channel_id=1, source_target_pairs={{0,1},{1,0},{2,3},{3,2},{4,5},{5,4},{6,7},{7,6},{8,9},{9,8},{10,11... | collective-permute-start | bytes 3538952 | tf_op jit(solution)/shard_map/ppermute | solution.py:274
  38.9 34.9 %collective-permute-start.6 = (f32[1,32,1280]{2,1,0:T(8,128)S(1)}, f32[1,32,1280]{2,1,0:T(8,128)S(1)}, u32[]{:S(2)}, u32[]{:S(2)}) collective-permute-start(f32[1,32,1280]{2,1,0:T(8,128)S(1)} %constant_dynamic-slice_fusion.2), channel_id=1, source_target_pairs={{0,2},{1,3},{2,0},{3,1},{4,6},{5,7},{6,4},{7,5},{8,10},{9,11},{10,... | collective-permute-start | bytes 491528 | tf_op jit(solution)/shard_map/ppermute | solution.py:274
  57.2 16.5 %copy-start.4 = (f32[2,32,1280]{2,1,0:T(8,128)S(1)}, f32[2,32,1280]{2,1,0:T(8,128)}, u32[]{:S(2)}) copy-start(f32[2,32,1280]{2,1,0:T(8,128)} %get-tuple-element.21) | copy-start | bytes 983044
  57.3 16.5 %collective-permute-start.12 = (f32[2,32,1280]{2,1,0:T(8,128)}, f32[2,32,1280]{2,1,0:T(8,128)S(1)}, u32[]{:S(2)}, u32[]{:S(2)}) collective-permute-start(f32[2,32,1280]{2,1,0:T(8,128)} %get-tuple-element.22), channel_id=1, source_target_pairs={{0,1},{1,0},{2,3},{3,2},{4,5},{5,4},{6,7},{7,6},{8,9},{9,8},{10,11... | collective-permute-start | bytes 983048 | tf_op jit(solution)/shard_map/ppermute | solution.py:274
  73.2 2.0 %copy-start.3 = (f32[2,32,1280]{2,1,0:T(8,128)S(1)}, f32[2,32,1280]{2,1,0:T(8,128)}, u32[]{:S(2)}) copy-start(f32[2,32,1280]{2,1,0:T(8,128)} %get-tuple-element.19) | copy-start | bytes 983044
  73.2 2.0 %collective-permute-start.8 = (f32[2,32,1280]{2,1,0:T(8,128)}, f32[2,32,1280]{2,1,0:T(8,128)S(1)}, u32[]{:S(2)}, u32[]{:S(2)}) collective-permute-start(f32[2,32,1280]{2,1,0:T(8,128)} %get-tuple-element.20), channel_id=1, source_target_pairs={{0,1},{1,0},{2,3},{3,2},{4,5},{5,4},{6,7},{7,6},{8,9},{9,8},{10,11... | collective-permute-start | bytes 983048 | tf_op jit(solution)/shard_map/ppermute | solution.py:274
  73.8 2.3 %copy-start.1 = (f32[3,2,32,1536]{3,2,1,0:T(8,128)S(1)}, f32[3,2,32,1536]{3,2,1,0:T(8,128)}, u32[]{:S(2)}) copy-start(f32[3,2,32,1536]{3,2,1,0:T(8,128)} %get-tuple-element.14) | copy-start | bytes 3538948
  73.9 7.1 %collective-permute-start.13 = (f32[1,32,1280]{2,1,0:T(8,128)S(1)}, f32[1,32,1280]{2,1,0:T(8,128)S(1)}, u32[]{:S(2)}, u32[]{:S(2)}) collective-permute-start(f32[1,32,1280]{2,1,0:T(8,128)S(1)} %constant_dynamic-slice_fusion), channel_id=1, source_target_pairs={{0,2},{1,3},{2,0},{3,1},{4,6},{5,7},{6,4},{7,5},{8,10},{9,11},{10,... | collective-permute-start | bytes 491528 | tf_op jit(solution)/shard_map/ppermute | solution.py:274
  75.3 9.2 %collective-permute-start.9 = (f32[1,32,1280]{2,1,0:T(8,128)S(1)}, f32[1,32,1280]{2,1,0:T(8,128)S(1)}, u32[]{:S(2)}, u32[]{:S(2)}) collective-permute-start(f32[1,32,1280]{2,1,0:T(8,128)S(1)} %constant_dynamic-slice_fusion.1), channel_id=1, source_target_pairs={{0,2},{1,3},{2,0},{3,1},{4,6},{5,7},{6,4},{7,5},{8,10},{9,11},{10,... | collective-permute-start | bytes 491528 | tf_op jit(solution)/shard_map/ppermute | solution.py:274
  76.3 19.9 %collective-permute-start.4 = (f32[3,1,32,1536]{3,2,0,1:T(8,128)S(1)}, f32[3,1,32,1536]{3,2,0,1:T(8,128)S(1)}, u32[]{:S(2)}, u32[]{:S(2)}) collective-permute-start(f32[3,1,32,1536]{3,2,0,1:T(8,128)S(1)} %constant_dynamic-slice_fusion.3), channel_id=1, source_target_pairs={{0,2},{1,3},{2,0},{3,1},{4,6},{5,7},{6,4},{7,5},{8,10},{9,11},{10,... | collective-permute-start | bytes 1769480 | tf_op jit(solution)/shard_map/ppermute | solution.py:274
  96.3 14.5 %copy-start = (f32[3,32,1536]{2,1,0:T(8,128)}, f32[3,32,1536]{2,1,0:T(8,128)S(1)}, u32[]{:S(2)}) copy-start(f32[3,32,1536]{2,1,0:T(8,128)S(1)} %add_bitcast_fusion.p_ref) | copy-start | bytes 1769476
  97.1 18.5 %collective-permute-start.10 = (f32[32,1408]{1,0:T(8,128)S(1)}, f32[32,1408]{1,0:T(8,128)S(1)}, u32[]{:S(2)}, u32[]{:S(2)}) collective-permute-start(f32[32,1408]{1,0:T(8,128)S(1)} %get-tuple-element.24), channel_id=1, source_target_pairs={{0,28},{4,0},{8,4},{12,8},{16,12},{20,16},{24,20},{28,24},{1,29},{... | collective-permute-start | bytes 540680 | tf_op jit(solution)/shard_map/ppermute | solution.py:269
  99.1 19.2 %collective-permute-start.14 = (f32[32,1408]{1,0:T(8,128)S(1)}, f32[32,1408]{1,0:T(8,128)S(1)}, u32[]{:S(2)}, u32[]{:S(2)}) collective-permute-start(f32[32,1408]{1,0:T(8,128)S(1)} %get-tuple-element.23), channel_id=1, source_target_pairs={{0,24},{4,28},{8,0},{12,4},{16,8},{20,12},{24,16},{28,20},{1,25},{... | collective-permute-start | bytes 540680 | tf_op jit(solution)/shard_map/ppermute | solution.py:269
  115.7 2.7 %copy-start.5 = (f32[32,1408]{1,0:T(8,128)}, f32[32,1408]{1,0:T(8,128)S(1)}, u32[]{:S(2)}) copy-start(f32[32,1408]{1,0:T(8,128)S(1)} %collective-permute-done.10.n1_ref) | copy-start | bytes 540676
  (4 other events, 3.3 us)

commit v2 on v0

v2 whole, which is shorter than its diff:
```python
import jax
import jax.numpy as jnp
from jax import lax
from jax.experimental import pallas as pl
from jax.experimental.pallas import tpu as pltpu
from jax.sharding import PartitionSpec as P

TLEN = 100
EPSILON = 1e-06
SIDE = 16
STEP = 32
EDGE = 128
MIB = 1024 * 1024
PAIRS = (TLEN + 2) // 2
TAPS = 2 * PAIRS + 1

VMEM = pl.BlockSpec(memory_space=pltpu.VMEM)
ANY = pl.BlockSpec(memory_space=pl.ANY)
HBM = pl.BlockSpec(memory_space=pltpu.HBM)
F32, BF16 = jnp.float32, jnp.bfloat16


def relayout(t_hbm, t_ref, v_ref, w, tall, mask, arrived):
    chans = v_ref.shape[1]
    wide = STEP * TLEN
    mask[...] = v_ref[...].astype(F32).T
    blank = jnp.zeros(w.shape[1:], w.dtype)
    w[0] = blank
    for tap in range(TLEN + 1, TAPS):
        w[tap] = blank

    def step(i, total):
        columns = pl.ds(pl.multiple_of(i * wide, wide), wide)
        channels = pl.ds(pl.multiple_of(i * STEP, STEP), STEP)
        pltpu.make_async_copy(t_hbm.at[:, columns], t_ref.at[:, columns], arrived.at[i]).wait()
        tall[...] = t_ref[:, columns].T.astype(F32)
        keep = mask[channels, :]

        def tap(l, total):
            kernel = tall[pl.ds(l, STEP, stride=TLEN), :] * keep
            w[l + 1, channels, :] = kernel.astype(w.dtype)
            return total + kernel * kernel

        return lax.fori_loop(0, TLEN, tap, total, unroll=10)

    total = lax.fori_loop(0, chans // STEP, step, jnp.zeros((STEP, w.shape[2]), F32))
    norm = jnp.sum(total, axis=0, keepdims=True)
    return jnp.broadcast_to(norm, (128, norm.shape[1])).T


def interleave(x_ref, h_ref, turned, windows, edge, open_at):
    chans, slab = x_ref.shape
    lanes = turned.shape[2]
    step = slab // SIDE
    spans = [slice(at, min(at + lanes, chans)) for at in range(0, chans, lanes)]
    for b, rows in enumerate(spans):
        turned[b, :slab, :rows.stop - rows.start] = x_ref[rows, :].T.astype(F32)
    edge.wait()
    follows = jnp.float32(1) if open_at is None else (lax.axis_index("tm") != open_at).astype(F32)
    for b, rows in enumerate(spans):
        turned[b, slab:, :rows.stop - rows.start] = h_ref[rows, :].T.astype(F32) * follows
    for a in range(windows.shape[0] // SIDE):
        for p in range(2):
            for b, rows in enumerate(spans):
                n = rows.stop - rows.start
                samples = turned[b, pl.ds(2 * a + p, SIDE, stride=step), :]
                at = p * chans + rows.start
                windows[a * SIDE:(a + 1) * SIDE, at:at + n] = samples[:, :n].astype(windows.dtype)


def correlate(w, windows, acc, flat):
    half, rows = acc.shape[1:]
    left = [windows[q * SIDE:q * SIDE + half, :] for q in range(PAIRS)]
    right = [jnp.concatenate([w[m + 1], w[m]], axis=1) for m in range(2 * PAIRS)]
    d = jnp.dot(jnp.concatenate(left, axis=1), jnp.concatenate(right, axis=0), preferred_element_type=F32)
    for r in range(2):
        acc[r] = d[:, r * rows:(r + 1) * rows]
    inner = half // SIDE
    for r in range(2):
        for b in range(SIDE):
            flat[pl.ds(2 * inner * b + r, inner, stride=2), :] = acc[r, pl.ds(b, inner, stride=SIDE), :]


def hand_out(rows_of, keep_ref, give_ref):
    mine = lax.axis_index("chan")
    piece = keep_ref.shape[-2]
    for d in range(2 * keep_ref.shape[0]):
        block = rows_of(pl.ds(pl.multiple_of((mine ^ d) * piece, piece), piece))
        (give_ref if d % 2 else keep_ref)[d // 2] = block


def traces(flat, norm, whole, keep_ref, give_ref):
    slab = flat.shape[0]
    whole[:, :slab] = flat[...].T
    whole[:, slab:] = norm
    hand_out(lambda rows: whole[rows, :], keep_ref, give_ref)


def power_kernel(x_hbm, h_ref, v_hbm, v1_ref, v2_ref, keep_ref, give_ref, x_ref, v0_ref, sems):
    copies = [pltpu.make_async_copy(v_hbm, v0_ref, sems.at[0]), pltpu.make_async_copy(x_hbm, x_ref, sems.at[1])]
    for copy in copies:
        copy.start()
    for copy in copies:
        copy.wait()
    slab = x_ref.shape[1]
    pieces, blocks, piece, wide = keep_ref.shape
    pieces *= 2
    mine = lax.axis_index("chan")
    valid = jnp.concatenate([
        r[pl.ds(pl.multiple_of((mine ^ d) * piece, piece), piece), :].astype(F32)
        for d in range(pieces) for r in (v0_ref, v1_ref, v2_ref)
    ], axis=0)
    count = jnp.sum(valid, axis=1, keepdims=True)
    valid = valid.astype(BF16)
    for at in range(0, wide, 128):
        part = x_ref[:, at:at + 128] if at < slab else h_ref[:, at - slab:at - slab + 128]
        square = jnp.square(part.astype(F32))
        high = square.astype(BF16)
        low = (square - high.astype(F32)).astype(BF16)
        total = jnp.dot(valid, high, preferred_element_type=F32) + jnp.dot(valid, low, preferred_element_type=F32)
        if at + 128 == wide:
            lane = lax.broadcasted_iota(jnp.int32, total.shape, 1)
            total = jnp.where(lane == 127, count, total)
        total = total.reshape(pieces, blocks, piece, 128)
        for d in range(pieces):
            (give_ref if d % 2 else keep_ref)[d // 2, :, :, at:at + 128] = total[d]


def relayout_kernel(t_hbm, v_hbm, w, norm_ref, t_ref, v_ref, tall, mask, arrived, sem):
    copy = pltpu.make_async_copy(v_hbm, v_ref, sem)
    copy.start()
    wide = STEP * TLEN
    for i in range(v_ref.shape[1] // STEP):
        columns = pl.ds(i * wide, wide)
        pltpu.make_async_copy(t_hbm.at[:, columns], t_ref.at[:, columns], arrived.at[i]).start()
    copy.wait()
    norm_ref[...] = relayout(t_hbm, t_ref, v_ref, w, tall, mask, arrived)


def slab_kernel(open_at, w, norm_ref, x_ref, next_hbm, keep_ref, give_ref, h_ref, turned, windows, acc, flat, whole, arrived):
    edge = pltpu.make_async_copy(next_hbm.at[:, pl.ds(0, EDGE)], h_ref, arrived)
    edge.start()
    interleave(x_ref, h_ref, turned, windows, edge, open_at)
    correlate(w, windows, acc, flat)
    traces(flat, norm_ref[...], whole, keep_ref, give_ref)


def scratch(chans, slab, rows):
    half = slab // 2
    return [
        pltpu.VMEM((-(-chans // 128), slab + EDGE, 128), F32),
        pltpu.VMEM((half + (PAIRS - 1) * SIDE, 2 * chans), BF16),
        pltpu.VMEM((2, half, rows), F32),
        pltpu.VMEM((slab, rows), F32),
        pltpu.VMEM((rows, slab + 128), F32),
    ]


def edge_kernel(x_hbm, out_ref, sem):
    copy = pltpu.make_async_copy(x_hbm.at[:, pl.ds(0, EDGE)], out_ref, sem)
    copy.start()
    copy.wait()


def edge_of(x):
    chans = x.shape[0]
    return pl.pallas_call(
        edge_kernel,
        in_specs=[HBM],
        out_specs=VMEM,
        out_shape=jax.ShapeDtypeStruct((chans, EDGE), x.dtype),
        scratch_shapes=[pltpu.SemaphoreType.DMA],
        compiler_params=pltpu.CompilerParams(vmem_limit_bytes=MIB),
        cost_estimate=pl.CostEstimate(flops=chans * 2 ** 26, bytes_accessed=4 * chans * EDGE, transcendentals=0),
    )(x)


def power_of(x, h, valids, pieces):
    chans, slab = x.shape
    rows = valids[0].shape[0]
    return pl.pallas_call(
        power_kernel,
        in_specs=[HBM, VMEM, HBM, VMEM, VMEM],
        out_specs=[VMEM] * 2,
        out_shape=[jax.ShapeDtypeStruct((pieces // 2, 3, rows // pieces, slab + EDGE), F32)] * 2,
        scratch_shapes=[pltpu.VMEM(x.shape, x.dtype), pltpu.VMEM(valids[0].shape, jnp.int32), pltpu.SemaphoreType.DMA((2,))],
        compiler_params=pltpu.CompilerParams(vmem_limit_bytes=12 * MIB),
        cost_estimate=pl.CostEstimate(flops=12 * rows * chans * slab, bytes_accessed=16 * rows * slab, transcendentals=0),
    )(x, h, *valids)


def tap_major(templates, valid):
    rows, chans = valid.shape
    return pl.pallas_call(
        relayout_kernel,
        in_specs=[HBM] * 2,
        out_specs=[VMEM] * 2,
        out_shape=[jax.ShapeDtypeStruct((TAPS, chans, rows), BF16), jax.ShapeDtypeStruct((rows, 128), F32)],
        scratch_shapes=[
            pltpu.VMEM(templates.shape, templates.dtype),
            pltpu.VMEM(valid.shape, valid.dtype),
            pltpu.VMEM((STEP * TLEN, rows), F32),
            pltpu.VMEM((chans, rows), F32),
            pltpu.SemaphoreType.DMA((chans // STEP,)),
            pltpu.SemaphoreType.DMA,
        ],
        compiler_params=pltpu.CompilerParams(vmem_limit_bytes=26 * MIB),
        cost_estimate=pl.CostEstimate(flops=0, bytes_accessed=4 * rows * chans * TLEN, transcendentals=0),
    )(templates, valid)


def correlated(w, norm, x, follows, open_at, pieces):
    chans, slab = x.shape
    rows = w.shape[2]
    return pl.pallas_call(
        lambda *refs: slab_kernel(open_at, *refs),
        in_specs=[VMEM, VMEM, VMEM, ANY],
        out_specs=[VMEM] * 2,
        out_shape=[jax.ShapeDtypeStruct((pieces // 2, rows // pieces, slab + 128), F32)] * 2,
        scratch_shapes=[pltpu.VMEM((chans, EDGE), x.dtype)] + scratch(chans, slab, rows) + [pltpu.SemaphoreType.DMA],
        compiler_params=pltpu.CompilerParams(vmem_limit_bytes=18 * MIB),
        cost_estimate=pl.CostEstimate(flops=3 * rows * chans * TLEN * slab, bytes_accessed=2 * rows * chans * TLEN, transcendentals=0),
    )(w, norm, x, follows)


def added(refs):
    total = refs[0][...]
    for ref in refs[1:]:
        total = total + ref[...]
    return total


def windowed(power, wide):
    sums = {1: power}
    for reach in (1, 2, 4, 8, 16, 32):
        sums[2 * reach] = sums[reach] + pltpu.roll(sums[reach], wide - reach, 1)
    return sums[64] + pltpu.roll(sums[32], wide - 64, 1) + pltpu.roll(sums[4], wide - 96, 1)


def scaled(num, esum, count):
    slab = esum.shape[1]
    norm = num[:, slab:slab + 1]
    return num[:, :slab] * jnp.sqrt(count * TLEN) * lax.rsqrt(esum * norm + EPSILON)


def early_kernel(parts, *refs):
    powers, num0, num1 = refs[:parts], refs[parts:2 * parts], refs[2 * parts:-3]
    out_ref, esum_ref, count_ref = refs[-3:]
    slab = out_ref.shape[2]
    wide = slab + EDGE
    num0 = [r.at[0] for r in num0[:2]] + list(num0[2:])
    for j in range(3):
        power = added([r.at[0, j] for r in powers[:2]] + [r.at[j] for r in powers[2:]])
        esum = windowed(power, wide)[:, :slab]
        count = power[:, wide - 1:]
        if j < 2:
            out_ref[j] = scaled(added((num0, num1)[j]), esum, count)
        else:
            esum_ref[...] = esum
            count_ref[...] = jnp.broadcast_to(count, count_ref.shape)


def early(powers, num0, num1):
    piece, wide = num1[0].shape
    slab = wide - 128
    parts = len(powers)
    return pl.pallas_call(
        lambda *refs: early_kernel(parts, *refs),
        in_specs=[VMEM] * (2 * parts + len(num1)),
        out_specs=[VMEM] * 3,
        out_shape=[jax.ShapeDtypeStruct((3, piece, slab), F32), jax.ShapeDtypeStruct((piece, slab), F32), jax.ShapeDtypeStruct((piece, 128), F32)],
        compiler_params=pltpu.CompilerParams(vmem_limit_bytes=12 * MIB),
    )(*powers, *num0, *num1)


def last_kernel(pieces, _, esum_ref, count_ref, *refs):
    parts, out_hbm, trace, sent = refs[:pieces], refs[pieces], refs[pieces + 1], refs[pieces + 2]
    trace[...] = scaled(added(parts), esum_ref[...], count_ref[:, :1])
    copy = pltpu.make_async_copy(trace, out_hbm.at[2], sent)
    copy.start()
    copy.wait()


def last(out, esum, count, parts):
    return pl.pallas_call(
        lambda *refs: last_kernel(len(parts), *refs),
        in_specs=[ANY] + [VMEM] * (2 + len(parts)),
        out_specs=ANY,
        out_shape=jax.ShapeDtypeStruct(out.shape, out.dtype),
        scratch_shapes=[pltpu.VMEM(esum.shape, F32), pltpu.SemaphoreType.DMA],
        input_output_aliases={0: 0},
        compiler_params=pltpu.CompilerParams(vmem_limit_bytes=4 * MIB),
    )(out, esum, count, *parts)


def sent(block, slabs, distance):
    n, m = lax.axis_size("tm"), lax.axis_size("chan")
    if distance == 0:
        return lax.ppermute(block, "tm", [(i, (i + slabs) % n) for i in range(n)]) if slabs else block
    if slabs == 0:
        return lax.ppermute(block, "chan", [(k, k ^ distance) for k in range(m)])
    route = [(i * m + k, (i + slabs) % n * m + (k ^ distance)) for i in range(n) for k in range(m)]
    return lax.ppermute(block, ("tm", "chan"), route)


together = lax.optimization_barrier


def local(data, templates, valid):
    pieces = lax.axis_size("chan")
    n = lax.axis_size("tm")
    others = range(1, pieces // 2)
    head = lax.ppermute(edge_of(data), "tm", [(i + 1, i) for i in range(n - 1)])
    valid1 = sent(valid, -1, 0)
    valid2 = sent(valid, -2, 0)
    w, norm = tap_major(templates, valid)
    w, head, valid1, valid2, moving = together((w, head, valid1, valid2, data))
    earlier = sent(moving, 1, 0)
    earliest = sent(moving, 2, 0)

    power_keep, power_give = power_of(data, head, (valid, valid1, valid2), pieces)
    head, power_give = together((head, power_give))
    power_got = sent(power_give, 0, 1)

    keep0, give0 = correlated(w, norm, data, head, None, pieces)
    give0, power_got = together((give0, power_got))
    got0 = sent(give0, 0, 1)
    powers = [power_keep[d] + power_got[d] for d in others]
    earlier, powers = together((earlier, powers))
    powers = [sent(part, 0, 2 * d) for d, part in zip(others, powers)]

    keep1, give1 = correlated(w, norm, earlier, data, 0, pieces)
    give1, got0, powers = together((give1, got0, powers))
    got1 = sent(give1, 0, 1)
    num0 = [keep0[d] + got0[d] for d in others]
    num1 = [keep1[d] + got1[d] for d in range(pieces // 2)]
    earliest, num0, num1 = together((earliest, num0, num1))
    num0 = [sent(part, 0, 2 * d) for d, part in zip(others, num0)]
    num1 = [sent(part, -1, 2 * d) for d, part in enumerate(num1)]

    keep2, give2 = correlated(w, norm, earliest, earlier, 1, pieces)
    give2, num1, num0 = together((give2, num1, num0))
    got2 = sent(give2, 0, 1)
    num2 = [keep2[d] + got2[d] for d in range(pieces // 2)]
    num2 = [sent(part, -2, 2 * d) for d, part in enumerate(num2)]
    out, esum, count = early([power_keep, power_got] + powers, [keep0, got0] + num0, num1)
    return last(out, esum, count, num2)


def solution(mesh):
    placed = (P("chan", "tm"), P("tm", "chan"), P("tm", "chan"))
    return jax.shard_map(
        local, mesh=mesh, in_specs=placed, out_specs=P(None, "chan", "tm"), check_vma=False
    )
```

time: 420 us -> 77.1 us (0.18); the launches traced: 414 us -> 77 us
  other arithmetic: 119 us -> 0.17 us
  waiting for transfers between devices: 106 us -> 14.5 us
  local copies, waits for them, and re-layouts: 90 us -> 2.34 us
  matrix products: 71.5 us -> 0 us
  Pallas kernels: 0 us -> 40.6 us
  between operations: 14.4 us -> 0.38 us
  starting transfers between devices: 13.3 us -> 19 us
    another operation x6 -> x0, other arithmetic: 107 us -> none  [the longest x3 104 us: window_energy(): lax.reduce_window(squares, jnp.float32(0.0), lax.add, (1, TLEN), (1, 1),...]
    unnamed x6 -> x0, waiting for transfers between devices: 99.6 us -> none
    conv_general_dilated x3 -> x0, matrix products: 67.6 us -> none  [block_terms(): lax.conv_general_dilated(segment[None], kernel, (1,), 'VALID', dimension_...]
    reshape x2 -> x0, local copies, waits for them, and re-layouts: 45.6 us -> none  [block_terms(): kernel = block.reshape(rows, chans, TLEN) * weights[:, :, None]]
    pallas_call x0 -> x8, Pallas kernels: none -> 40.6 us  [the longest x3 31 us: correlated(): pl.pallas_call(lambda *refs: slab_kernel(open_at, *refs), in_specs=[VMEM,...]
    unnamed x25 -> x8, local copies, waits for them, and re-layouts: 16.4 us -> 2.34 us
    mul x2 -> x0, local copies, waits for them, and re-layouts: 13.5 us -> none  [block_terms(): kernel = block.reshape(rows, chans, TLEN) * weights[:, :, None]]
    ppermute x5 -> x15, waiting for transfers between devices: 6.17 us -> 14.5 us  [the longest x6 7.77 us: sent(): lax.ppermute(block, 'tm', [(i, (i + slabs) % n) for i in range(n)])]
  transfers between devices with their start and end apart: 8 -> 15, of which waited for: 3 -> 5; matrix products, arithmetic and copies ran while one was open for 66% -> 0% of each run, Pallas kernels for 0% -> 52%
where the time goes in v2:
time: 77.1 us; the launch traced here: 77 us
  Pallas kernels  40.6 us (53%)
  starting transfers between devices  19 us (25%)
  waiting for transfers between devices  14.5 us (19%)
  local copies, waits for them, and re-layouts  2.34 us (3%)
    pallas_call x3, Pallas kernels, correlated(): pl.pallas_call(lambda *refs: slab_kernel(open_at, *refs), in_specs=[VMEM,...  31 us
    ppermute x6, starting transfers between devices, sent(): lax.ppermute(block, 'tm', [(i, (i + slabs) % n) for i in range(n)])  10.9 us
    ppermute x6, waiting for transfers between devices, sent(): lax.ppermute(block, 'tm', [(i, (i + slabs) % n) for i in range(n)])  7.77 us
    pallas_call x1, Pallas kernels, tap_major(): pl.pallas_call(relayout_kernel, in_specs=[HBM] * 2, out_specs=[VMEM] * 2,...  5.13 us
    ppermute x2, waiting for transfers between devices, sent(): return lax.ppermute(block, ('tm', 'chan'), route)  3.79 us
    ppermute x2, starting transfers between devices, sent(): return lax.ppermute(block, ('tm', 'chan'), route)  3.79 us
    ppermute x6, waiting for transfers between devices, sent(): return lax.ppermute(block, 'chan', [(k, k ^ distance) for k in range(m)])  2.95 us
    ppermute x6, starting transfers between devices, sent(): return lax.ppermute(block, 'chan', [(k, k ^ distance) for k in range(m)])  2.72 us
  transfers between devices with their start and end apart: 15, of which 5 were waited for; matrix products, arithmetic and copies ran while one was open for 0% of the time, Pallas kernels for 52%

profile of v2, /device:TPU:0, one launch (start us, length us, event | category | flops | bytes accessed | tf_op | source)
XLA Modules:
  0.0 77.0 jit_solution(7387354973251372936)
XLA Ops:
  0.0 6.0 %collective-permute-start.1 = (s32[128,256]{1,0:T(8,128)}, s32[128,256]{1,0:T(8,128)S(1)}, u32[]{:S(2)}, u32[]{:S(2)}) collective-permute-start(s32[128,256]{1,0:T(8,128)} %v_hbm.3), channel_id=1, source_target_pairs={{0,28},{4,0},{8,4},{12,8},{16,12},{20,16},{24,20},{28,24},{1,29},{... | collective-permute-start | bytes 393224 | tf_op jit(solution)/shard_map/ppermute | solution.py:299
  6.4 1.1 %copy-done.2 = bf16[256,1280]{1,0:T(8,128)(2,1)S(1)} copy-done((bf16[256,1280]{1,0:T(8,128)(2,1)S(1)}, bf16[256,1280]{1,0:T(8,128)(2,1)}, u32[]{:S(2)}) %copy-start.2) | copy-done | bytes 655384
  7.6 1.6 %collective-permute-start = (bf16[256,128]{1,0:T(8,128)(2,1)S(1)}, bf16[256,128]{1,0:T(8,128)(2,1)S(1)}, u32[]{:S(2)}, u32[]{:S(2)}) collective-permute-start(bf16[256,128]{1,0:T(8,128)(2,1)S(1)} %shard_map.38), channel_id=1, source_target_pairs={{4,0},{8,4},{12,8},{16,12},{20,16},{24,20},{28,24},{5,1},{9,5},{13... | collective-permute-start | bytes 196616 | tf_op jit(solution)/shard_map/ppermute | solution.py:313
  9.1 1.2 %copy-done = bf16[128,25600]{1,0:T(8,128)(2,1)S(1)} copy-done((bf16[128,25600]{1,0:T(8,128)(2,1)S(1)}, bf16[128,25600]{1,0:T(8,128)(2,1)}, u32[]{:S(2)}) %copy-start) | copy-done | bytes 6553624
  10.4 5.1 %shard_map.37 = (bf16[103,256,128]{2,1,0:T(8,128)(2,1)S(1)}, f32[128,128]{1,0:T(8,128)S(1)}) custom-call(bf16[128,25600]{1,0:T(8,128)(2,1)S(1)} %copy-done, s32[128,256]{1,0:T(8,128)S(1)} %copy-done.1), custom_call_target="tpu_custom_call" | custom-call | bytes 13107200 | tf_op jit(solution)/shard_map/pallas_call | solution.py:194
  15.6 1.5 %collective-permute-start.4 = (bf16[256,1280]{1,0:T(8,128)(2,1)S(1)}, bf16[256,1280]{1,0:T(8,128)(2,1)S(1)}, u32[]{:S(2)}, u32[]{:S(2)}) collective-permute-start(bf16[256,1280]{1,0:T(8,128)(2,1)S(1)} %copy-done.3), channel_id=1, source_target_pairs={{0,4},{4,8},{8,12},{12,16},{16,20},{20,24},{24,28},{28,0},{1,5},{5... | collective-permute-start | bytes 1966088 | tf_op jit(solution)/shard_map/ppermute | solution.py:299
  17.1 1.6 %collective-permute-start.7 = (bf16[256,1280]{1,0:T(8,128)(2,1)S(1)}, bf16[256,1280]{1,0:T(8,128)(2,1)S(1)}, u32[]{:S(2)}, u32[]{:S(2)}) collective-permute-start(bf16[256,1280]{1,0:T(8,128)(2,1)S(1)} %copy-done.3), channel_id=1, source_target_pairs={{0,8},{4,12},{8,16},{12,20},{16,24},{20,28},{24,0},{28,4},{1,9},{5... | collective-permute-start | bytes 1966088 | tf_op jit(solution)/shard_map/ppermute | solution.py:299
  18.6 1.7 %shard_map.39 = (f32[2,3,32,1408]{3,2,1,0:T(8,128)S(1)}, f32[2,3,32,1408]{3,2,1,0:T(8,128)S(1)}) custom-call(bf16[256,1280]{1,0:T(8,128)(2,1)S(1)} %copy-done.3, bf16[256,128]{1,0:T(8,128)(2,1)S(1)} %collective-permute-done.h_ref.refs_3_, s32[128,256]{1,0:T(8,128)S(1)} %copy-done.1, s32[128,256]{1,0:T(8,128)S(1)} %collective-permute-done.1.v1_ref, ...), custom_call_target="tpu_custom_call" | custom-call | flops 503316480 | bytes 2621440 | tf_op jit(solution)/shard_map/pallas_call | solution.py:181
  20.4 10.4 %shard_map.40 = (f32[2,32,1408]{2,1,0:T(8,128)S(1)}, f32[2,32,1408]{2,1,0:T(8,128)S(1)}) custom-call(bf16[103,256,128]{2,1,0:T(8,128)(2,1)S(1)} %get-tuple-element.45.refs_0_, f32[128,128]{1,0:T(8,128)S(1)} %get-tuple-element.46.refs_1_, bf16[256,1280]{1,0:T(8,128)(2,1)S(1)} %copy-done.3, bf16[256,128]{1,0:T(8,128)(2,1)S(1)} %collective-permute-done.h_ref.refs_3_), custom_call_target="tpu_custom_call" | custom-call | flops 12582912000 | bytes 6553600 | tf_op jit(solution)/shard_map/pallas_call | solution.py:215
  30.9 5.1 %collective-permute-done.4.refs_2_.refs_3_ = bf16[256,1280]{1,0:T(8,128)(2,1)S(1)} collective-permute-done((bf16[256,1280]{1,0:T(8,128)(2,1)S(1)}, bf16[256,1280]{1,0:T(8,128)(2,1)S(1)}, u32[]{:S(2)}, u32[]{:S(2)}) %collective-permute-start.4) | collective-permute-done | bytes 655392 | tf_op jit(solution)/shard_map/ppermute | solution.py:299
  36.0 1.5 %collective-permute-start.6 = (f32[3,32,1408]{2,1,0:T(8,128)S(1)}, f32[3,32,1408]{2,1,0:T(8,128)S(1)}, u32[]{:S(2)}, u32[]{:S(2)}) collective-permute-start(f32[3,32,1408]{2,1,0:T(8,128)S(1)} %add_bitcast_fusion), channel_id=1, source_target_pairs={{0,2},{1,3},{2,0},{3,1},{4,6},{5,7},{6,4},{7,5},{8,10},{9,11},{10,... | collective-permute-start | bytes 1622024 | tf_op jit(solution)/shard_map/ppermute | solution.py:301
  37.5 10.4 %shard_map.41 = (f32[2,32,1408]{2,1,0:T(8,128)S(1)}, f32[2,32,1408]{2,1,0:T(8,128)S(1)}) custom-call(bf16[103,256,128]{2,1,0:T(8,128)(2,1)S(1)} %get-tuple-element.45.refs_0_, f32[128,128]{1,0:T(8,128)S(1)} %get-tuple-element.46.refs_1_, bf16[256,1280]{1,0:T(8,128)(2,1)S(1)} %collective-permute-done.4.refs_2_.refs_3_, bf16[256,1280]{1,0:T(8,128)(2,1)S(1)} %copy-done.3), custom_call_target="tpu_custom_call" | custom-call | flops 12582912000 | bytes 6553600 | tf_op jit(solution)/shard_map/pallas_call | solution.py:215
  47.9 0.6 collective-permute-start.8
  48.5 1.3 %collective-permute-done.8 = f32[2,32,1408]{2,1,0:T(8,128)S(1)} collective-permute-done((f32[2,32,1408]{2,1,0:T(8,128)S(1)}, f32[2,32,1408]{2,1,0:T(8,128)S(1)}, u32[]{:S(2)}, u32[]{:S(2)}) %collective-permute-start.8) | collective-permute-done | bytes 360480 | tf_op jit(solution)/shard_map/ppermute | solution.py:301
  49.8 1.8 %collective-permute-start.10 = (f32[32,1408]{1,0:T(8,128)S(1)}, f32[32,1408]{1,0:T(8,128)S(1)}, u32[]{:S(2)}, u32[]{:S(2)}) collective-permute-start(f32[32,1408]{1,0:T(8,128)S(1)} %get-tuple-element.65), channel_id=1, source_target_pairs={{0,30},{1,31},{2,28},{3,29},{4,2},{5,3},{6,0},{7,1},{8,6},{9,7},{1... | collective-permute-start | bytes 540680 | tf_op jit(solution)/shard_map/ppermute | solution.py:303
  51.6 0.5 collective-permute-start.11
  52.6 10.2 %shard_map.42 = (f32[2,32,1408]{2,1,0:T(8,128)S(1)}, f32[2,32,1408]{2,1,0:T(8,128)S(1)}) custom-call(bf16[103,256,128]{2,1,0:T(8,128)(2,1)S(1)} %get-tuple-element.45.refs_0_, f32[128,128]{1,0:T(8,128)S(1)} %get-tuple-element.46.refs_1_, bf16[256,1280]{1,0:T(8,128)(2,1)S(1)} %collective-permute-done.7.refs_2_, ...), custom_call_target="tpu_custom_call" | custom-call | flops 12582912000 | bytes 6553600 | tf_op jit(solution)/shard_map/pallas_call | solution.py:215
  62.8 1.7 %collective-permute-done.12 = f32[2,32,1408]{2,1,0:T(8,128)S(1)} collective-permute-done((f32[2,32,1408]{2,1,0:T(8,128)S(1)}, f32[2,32,1408]{2,1,0:T(8,128)S(1)}, u32[]{:S(2)}, u32[]{:S(2)}) %collective-permute-start.12) | collective-permute-done | bytes 360480 | tf_op jit(solution)/shard_map/ppermute | solution.py:301
  64.5 1.0 %collective-permute-start.13 = (f32[32,1408]{1,0:T(8,128)S(1)}, f32[32,1408]{1,0:T(8,128)S(1)}, u32[]{:S(2)}, u32[]{:S(2)}) collective-permute-start(f32[32,1408]{1,0:T(8,128)S(1)} %get-tuple-element.76), channel_id=1, source_target_pairs={{0,24},{4,28},{8,0},{12,4},{16,8},{20,12},{24,16},{28,20},{1,25},{... | collective-permute-start | bytes 540680 | tf_op jit(solution)/shard_map/ppermute | solution.py:299
  65.5 2.0 %collective-permute-start.14 = (f32[32,1408]{1,0:T(8,128)S(1)}, f32[32,1408]{1,0:T(8,128)S(1)}, u32[]{:S(2)}, u32[]{:S(2)}) collective-permute-start(f32[32,1408]{1,0:T(8,128)S(1)} %get-tuple-element.75), channel_id=1, source_target_pairs={{0,26},{1,27},{2,24},{3,25},{4,30},{5,31},{6,28},{7,29},{8,2},{9,3... | collective-permute-start | bytes 540680 | tf_op jit(solution)/shard_map/ppermute | solution.py:303
  67.5 2.0 %shard_map.43 = (f32[3,32,1280]{2,1,0:T(8,128)}, f32[32,1280]{1,0:T(8,128)S(1)}, f32[32,128]{1,0:T(8,128)S(1)}) custom-call(f32[2,3,32,1408]{3,2,1,0:T(8,128)S(1)} %get-tuple-element.44.refs_0_, f32[2,3,32,1408]{3,2,1,0:T(8,128)S(1)} %collective-permute-done.3.refs_1_, f32[3,32,1408]{2,1,0:T(8,128)S(1)} %collective-permute-done.6.refs_2_, ...), custom_call_target="tpu_custom_call" | custom-call | tf_op jit(solution)/shard_map/pallas_call | solution.py:267
  69.6 2.7 %collective-permute-done.13.refs_3_ = f32[32,1408]{1,0:T(8,128)S(1)} collective-permute-done((f32[32,1408]{1,0:T(8,128)S(1)}, f32[32,1408]{1,0:T(8,128)S(1)}, u32[]{:S(2)}, u32[]{:S(2)}) %collective-permute-start.13) | collective-permute-done | bytes 180256 | tf_op jit(solution)/shard_map/ppermute | solution.py:299
  72.2 3.8 %collective-permute-done.14.refs_4_ = f32[32,1408]{1,0:T(8,128)S(1)} collective-permute-done((f32[32,1408]{1,0:T(8,128)S(1)}, f32[32,1408]{1,0:T(8,128)S(1)}, u32[]{:S(2)}, u32[]{:S(2)}) %collective-permute-start.14) | collective-permute-done | bytes 180256 | tf_op jit(solution)/shard_map/ppermute | solution.py:303
  76.0 0.8 %shard_map.44 = f32[3,32,1280]{2,1,0:T(8,128)} custom-call(f32[3,32,1280]{2,1,0:T(8,128)} %get-tuple-element.70.refs_0_, f32[32,1280]{1,0:T(8,128)S(1)} %get-tuple-element.71.refs_1_, f32[32,128]{1,0:T(8,128)S(1)} %get-tuple-element.72.refs_2_, f32[32,1408]{1,0:T(8,128)S(1)} %collective-permute-done.13.refs_3_, ...), custom_call_target="tpu_custom_call", output_to_operand_aliasing={{}: (0, {})} | custom-call | tf_op jit(solution)/shard_map/pallas_call | solution.py:285
  (26 shorter events, 1.3 us)
Async XLA Ops:
  0.0 9.1 %copy-start.1 = (s32[128,256]{1,0:T(8,128)S(1)}, s32[128,256]{1,0:T(8,128)}, u32[]{:S(2)}) copy-start(s32[128,256]{1,0:T(8,128)} %v_hbm.3) | copy-start | bytes 393220
  0.0 15.5 %collective-permute-start.1 = (s32[128,256]{1,0:T(8,128)}, s32[128,256]{1,0:T(8,128)S(1)}, u32[]{:S(2)}, u32[]{:S(2)}) collective-permute-start(s32[128,256]{1,0:T(8,128)} %v_hbm.3), channel_id=1, source_target_pairs={{0,28},{4,0},{8,4},{12,8},{16,12},{20,16},{24,20},{28,24},{1,29},{... | collective-permute-start | bytes 393224 | tf_op jit(solution)/shard_map/ppermute | solution.py:299
  6.0 9.6 %collective-permute-start.2 = (s32[128,256]{1,0:T(8,128)}, s32[128,256]{1,0:T(8,128)S(1)}, u32[]{:S(2)}, u32[]{:S(2)}) collective-permute-start(s32[128,256]{1,0:T(8,128)} %v_hbm.3), channel_id=1, source_target_pairs={{0,24},{4,28},{8,0},{12,4},{16,8},{20,12},{24,16},{28,20},{1,25},{... | collective-permute-start | bytes 393224 | tf_op jit(solution)/shard_map/ppermute | solution.py:299
  6.4 1.1 %copy-start.2 = (bf16[256,1280]{1,0:T(8,128)(2,1)S(1)}, bf16[256,1280]{1,0:T(8,128)(2,1)}, u32[]{:S(2)}) copy-start(bf16[256,1280]{1,0:T(8,128)(2,1)} %refs_3_.1) | copy-start | bytes 1966084
  7.5 2.9 %copy-start = (bf16[128,25600]{1,0:T(8,128)(2,1)S(1)}, bf16[128,25600]{1,0:T(8,128)(2,1)}, u32[]{:S(2)}) copy-start(bf16[128,25600]{1,0:T(8,128)(2,1)} %t_hbm.1) | copy-start | bytes 19660804
  7.5 8.0 %copy-start.3 = (bf16[256,1280]{1,0:T(8,128)(2,1)S(1)}, bf16[256,1280]{1,0:T(8,128)(2,1)}, u32[]{:S(2)}) copy-start(bf16[256,1280]{1,0:T(8,128)(2,1)} %refs_3_.1) | copy-start | bytes 1966084
  7.6 8.0 %collective-permute-start = (bf16[256,128]{1,0:T(8,128)(2,1)S(1)}, bf16[256,128]{1,0:T(8,128)(2,1)S(1)}, u32[]{:S(2)}, u32[]{:S(2)}) collective-permute-start(bf16[256,128]{1,0:T(8,128)(2,1)S(1)} %shard_map.38), channel_id=1, source_target_pairs={{4,0},{8,4},{12,8},{16,12},{20,16},{24,20},{28,24},{5,1},{9,5},{13... | collective-permute-start | bytes 196616 | tf_op jit(solution)/shard_map/ppermute | solution.py:313
  15.6 20.4 %collective-permute-start.4 = (bf16[256,1280]{1,0:T(8,128)(2,1)S(1)}, bf16[256,1280]{1,0:T(8,128)(2,1)S(1)}, u32[]{:S(2)}, u32[]{:S(2)}) collective-permute-start(bf16[256,1280]{1,0:T(8,128)(2,1)S(1)} %copy-done.3), channel_id=1, source_target_pairs={{0,4},{4,8},{8,12},{12,16},{16,20},{20,24},{24,28},{28,0},{1,5},{5... | collective-permute-start | bytes 1966088 | tf_op jit(solution)/shard_map/ppermute | solution.py:299
  17.1 32.8 %collective-permute-start.7 = (bf16[256,1280]{1,0:T(8,128)(2,1)S(1)}, bf16[256,1280]{1,0:T(8,128)(2,1)S(1)}, u32[]{:S(2)}, u32[]{:S(2)}) collective-permute-start(bf16[256,1280]{1,0:T(8,128)(2,1)S(1)} %copy-done.3), channel_id=1, source_target_pairs={{0,8},{4,12},{8,16},{12,20},{16,24},{20,28},{24,0},{28,4},{1,9},{5... | collective-permute-start | bytes 1966088 | tf_op jit(solution)/shard_map/ppermute | solution.py:299
  20.3 10.5 %collective-permute-start.3 = (f32[2,3,32,1408]{3,2,1,0:T(8,128)S(1)}, f32[2,3,32,1408]{3,2,1,0:T(8,128)S(1)}, u32[]{:S(2)}, u32[]{:S(2)}) collective-permute-start(f32[2,3,32,1408]{3,2,1,0:T(8,128)S(1)} %get-tuple-element.50), channel_id=1, source_target_pairs={{0,1},{1,0},{2,3},{3,2},{4,5},{5,4},{6,7},{7,6},{8,9},{9,8},{10,11... | collective-permute-start | bytes 3244040 | tf_op jit(solution)/shard_map/ppermute | solution.py:301
  36.0 11.9 %collective-permute-start.6 = (f32[3,32,1408]{2,1,0:T(8,128)S(1)}, f32[3,32,1408]{2,1,0:T(8,128)S(1)}, u32[]{:S(2)}, u32[]{:S(2)}) collective-permute-start(f32[3,32,1408]{2,1,0:T(8,128)S(1)} %add_bitcast_fusion), channel_id=1, source_target_pairs={{0,2},{1,3},{2,0},{3,1},{4,6},{5,7},{6,4},{7,5},{8,10},{9,11},{10,... | collective-permute-start | bytes 1622024 | tf_op jit(solution)/shard_map/ppermute | solution.py:301
  37.5 10.4 %collective-permute-start.5 = (f32[2,32,1408]{2,1,0:T(8,128)S(1)}, f32[2,32,1408]{2,1,0:T(8,128)S(1)}, u32[]{:S(2)}, u32[]{:S(2)}) collective-permute-start(f32[2,32,1408]{2,1,0:T(8,128)S(1)} %get-tuple-element.55), channel_id=1, source_target_pairs={{0,1},{1,0},{2,3},{3,2},{4,5},{5,4},{6,7},{7,6},{8,9},{9,8},{10,11... | collective-permute-start | bytes 1081352 | tf_op jit(solution)/shard_map/ppermute | solution.py:301
  47.9 1.9 %collective-permute-start.8 = (f32[2,32,1408]{2,1,0:T(8,128)S(1)}, f32[2,32,1408]{2,1,0:T(8,128)S(1)}, u32[]{:S(2)}, u32[]{:S(2)}) collective-permute-start(f32[2,32,1408]{2,1,0:T(8,128)S(1)} %get-tuple-element.61), channel_id=1, source_target_pairs={{0,1},{1,0},{2,3},{3,2},{4,5},{5,4},{6,7},{7,6},{8,9},{9,8},{10,11... | collective-permute-start | bytes 1081352 | tf_op jit(solution)/shard_map/ppermute | solution.py:301
  49.8 12.9 %collective-permute-start.10 = (f32[32,1408]{1,0:T(8,128)S(1)}, f32[32,1408]{1,0:T(8,128)S(1)}, u32[]{:S(2)}, u32[]{:S(2)}) collective-permute-start(f32[32,1408]{1,0:T(8,128)S(1)} %get-tuple-element.65), channel_id=1, source_target_pairs={{0,30},{1,31},{2,28},{3,29},{4,2},{5,3},{6,0},{7,1},{8,6},{9,7},{1... | collective-permute-start | bytes 540680 | tf_op jit(solution)/shard_map/ppermute | solution.py:303
  51.6 11.1 %collective-permute-start.11 = (f32[32,1408]{1,0:T(8,128)S(1)}, f32[32,1408]{1,0:T(8,128)S(1)}, u32[]{:S(2)}, u32[]{:S(2)}) collective-permute-start(f32[32,1408]{1,0:T(8,128)S(1)} %add_bitcast_fusion.1), channel_id=1, source_target_pairs={{0,2},{1,3},{2,0},{3,1},{4,6},{5,7},{6,4},{7,5},{8,10},{9,11},{10,... | collective-permute-start | bytes 540680 | tf_op jit(solution)/shard_map/ppermute | solution.py:301
  52.1 10.6 %collective-permute-start.9 = (f32[32,1408]{1,0:T(8,128)S(1)}, f32[32,1408]{1,0:T(8,128)S(1)}, u32[]{:S(2)}, u32[]{:S(2)}) collective-permute-start(f32[32,1408]{1,0:T(8,128)S(1)} %get-tuple-element.64), channel_id=1, source_target_pairs={{0,28},{4,0},{8,4},{12,8},{16,12},{20,16},{24,20},{28,24},{1,29},{... | collective-permute-start | bytes 540680 | tf_op jit(solution)/shard_map/ppermute | solution.py:299
  62.7 1.7 %collective-permute-start.12 = (f32[2,32,1408]{2,1,0:T(8,128)S(1)}, f32[2,32,1408]{2,1,0:T(8,128)S(1)}, u32[]{:S(2)}, u32[]{:S(2)}) collective-permute-start(f32[2,32,1408]{2,1,0:T(8,128)S(1)} %get-tuple-element.74), channel_id=1, source_target_pairs={{0,1},{1,0},{2,3},{3,2},{4,5},{5,4},{6,7},{7,6},{8,9},{9,8},{10,11... | collective-permute-start | bytes 1081352 | tf_op jit(solution)/shard_map/ppermute | solution.py:301
  64.5 7.7 %collective-permute-start.13 = (f32[32,1408]{1,0:T(8,128)S(1)}, f32[32,1408]{1,0:T(8,128)S(1)}, u32[]{:S(2)}, u32[]{:S(2)}) collective-permute-start(f32[32,1408]{1,0:T(8,128)S(1)} %get-tuple-element.76), channel_id=1, source_target_pairs={{0,24},{4,28},{8,0},{12,4},{16,8},{20,12},{24,16},{28,20},{1,25},{... | collective-permute-start | bytes 540680 | tf_op jit(solution)/shard_map/ppermute | solution.py:299
  65.5 10.5 %collective-permute-start.14 = (f32[32,1408]{1,0:T(8,128)S(1)}, f32[32,1408]{1,0:T(8,128)S(1)}, u32[]{:S(2)}, u32[]{:S(2)}) collective-permute-start(f32[32,1408]{1,0:T(8,128)S(1)} %get-tuple-element.75), channel_id=1, source_target_pairs={{0,26},{1,27},{2,24},{3,25},{4,30},{5,31},{6,28},{7,29},{8,2},{9,3... | collective-permute-start | bytes 540680 | tf_op jit(solution)/shard_map/ppermute | solution.py:303

commit v3 on v2

--- a/solution.py
+++ b/solution.py
@@ -8,7 +8,7 @@
 TLEN = 100
 EPSILON = 1e-06
 SIDE = 16
-STEP = 32
+STEP = 64
 EDGE = 128
 MIB = 1024 * 1024
 PAIRS = (TLEN + 2) // 2
@@ -20,7 +20,7 @@
 F32, BF16 = jnp.float32, jnp.bfloat16
 
 
-def relayout(t_hbm, t_ref, v_ref, w, tall, mask, arrived):
+def relayout(t_ref, v_ref, w, tall, mask):
     chans = v_ref.shape[1]
     wide = STEP * TLEN
     mask[...] = v_ref[...].astype(F32).T
@@ -32,7 +32,6 @@
     def step(i, total):
         columns = pl.ds(pl.multiple_of(i * wide, wide), wide)
         channels = pl.ds(pl.multiple_of(i * STEP, STEP), STEP)
-        pltpu.make_async_copy(t_hbm.at[:, columns], t_ref.at[:, columns], arrived.at[i]).wait()
         tall[...] = t_ref[:, columns].T.astype(F32)
         keep = mask[channels, :]
 
@@ -41,24 +40,23 @@
             w[l + 1, channels, :] = kernel.astype(w.dtype)
             return total + kernel * kernel
 
-        return lax.fori_loop(0, TLEN, tap, total, unroll=10)
+        return lax.fori_loop(0, TLEN, tap, total, unroll=50)
 
     total = lax.fori_loop(0, chans // STEP, step, jnp.zeros((STEP, w.shape[2]), F32))
     norm = jnp.sum(total, axis=0, keepdims=True)
     return jnp.broadcast_to(norm, (128, norm.shape[1])).T
 
 
-def interleave(x_ref, h_ref, turned, windows, edge, open_at):
+def interleave(x_ref, next_ref, turned, windows, open_at):
     chans, slab = x_ref.shape
     lanes = turned.shape[2]
     step = slab // SIDE
     spans = [slice(at, min(at + lanes, chans)) for at in range(0, chans, lanes)]
     for b, rows in enumerate(spans):
         turned[b, :slab, :rows.stop - rows.start] = x_ref[rows, :].T.astype(F32)
-    edge.wait()
     follows = jnp.float32(1) if open_at is None else (lax.axis_index("tm") != open_at).astype(F32)
     for b, rows in enumerate(spans):
-        turned[b, slab:, :rows.stop - rows.start] = h_ref[rows, :].T.astype(F32) * follows
+        turned[b, slab:, :rows.stop - rows.start] = next_ref[rows, :EDGE].T.astype(F32) * follows
     for a in range(windows.shape[0] // SIDE):
         for p in range(2):
             for b, rows in enumerate(spans):
@@ -96,12 +94,7 @@
     hand_out(lambda rows: whole[rows, :], keep_ref, give_ref)
 
 
-def power_kernel(x_hbm, h_ref, v_hbm, v1_ref, v2_ref, keep_ref, give_ref, x_ref, v0_ref, sems):
-    copies = [pltpu.make_async_copy(v_hbm, v0_ref, sems.at[0]), pltpu.make_async_copy(x_hbm, x_ref, sems.at[1])]
-    for copy in copies:
-        copy.start()
-    for copy in copies:
-        copy.wait()
+def power_kernel(x_ref, h_ref, v0_ref, v1_ref, v2_ref, keep_ref, give_ref):
     slab = x_ref.shape[1]
     pieces, blocks, piece, wide = keep_ref.shape
     pieces *= 2
@@ -126,21 +119,12 @@
             (give_ref if d % 2 else keep_ref)[d // 2, :, :, at:at + 128] = total[d]
 
 
-def relayout_kernel(t_hbm, v_hbm, w, norm_ref, t_ref, v_ref, tall, mask, arrived, sem):
-    copy = pltpu.make_async_copy(v_hbm, v_ref, sem)
-    copy.start()
-    wide = STEP * TLEN
-    for i in range(v_ref.shape[1] // STEP):
-        columns = pl.ds(i * wide, wide)
-        pltpu.make_async_copy(t_hbm.at[:, columns], t_ref.at[:, columns], arrived.at[i]).start()
-    copy.wait()
-    norm_ref[...] = relayout(t_hbm, t_ref, v_ref, w, tall, mask, arrived)
-
-
-def slab_kernel(open_at, w, norm_ref, x_ref, next_hbm, keep_ref, give_ref, h_ref, turned, windows, acc, flat, whole, arrived):
-    edge = pltpu.make_async_copy(next_hbm.at[:, pl.ds(0, EDGE)], h_ref, arrived)
-    edge.start()
-    interleave(x_ref, h_ref, turned, windows, edge, open_at)
+def relayout_kernel(t_ref, v_ref, w, norm_ref, tall, mask):
+    norm_ref[...] = relayout(t_ref, v_ref, w, tall, mask)
+
+
+def slab_kernel(open_at, w, norm_ref, x_ref, next_ref, keep_ref, give_ref, turned, windows, acc, flat, whole):
+    interleave(x_ref, next_ref, turned, windows, open_at)
     correlate(w, windows, acc, flat)
     traces(flat, norm_ref[...], whole, keep_ref, give_ref)
 
@@ -180,10 +164,9 @@
     rows = valids[0].shape[0]
     return pl.pallas_call(
         power_kernel,
-        in_specs=[HBM, VMEM, HBM, VMEM, VMEM],
+        in_specs=[VMEM] * 5,
         out_specs=[VMEM] * 2,
         out_shape=[jax.ShapeDtypeStruct((pieces // 2, 3, rows // pieces, slab + EDGE), F32)] * 2,
-        scratch_shapes=[pltpu.VMEM(x.shape, x.dtype), pltpu.VMEM(valids[0].shape, jnp.int32), pltpu.SemaphoreType.DMA((2,))],
         compiler_params=pltpu.CompilerParams(vmem_limit_bytes=12 * MIB),
         cost_estimate=pl.CostEstimate(flops=12 * rows * chans * slab, bytes_accessed=16 * rows * slab, transcendentals=0),
     )(x, h, *valids)
@@ -193,17 +176,10 @@
     rows, chans = valid.shape
     return pl.pallas_call(
         relayout_kernel,
-        in_specs=[HBM] * 2,
+        in_specs=[VMEM] * 2,
         out_specs=[VMEM] * 2,
         out_shape=[jax.ShapeDtypeStruct((TAPS, chans, rows), BF16), jax.ShapeDtypeStruct((rows, 128), F32)],
-        scratch_shapes=[
-            pltpu.VMEM(templates.shape, templates.dtype),
-            pltpu.VMEM(valid.shape, valid.dtype),
-            pltpu.VMEM((STEP * TLEN, rows), F32),
-            pltpu.VMEM((chans, rows), F32),
-            pltpu.SemaphoreType.DMA((chans // STEP,)),
-            pltpu.SemaphoreType.DMA,
-        ],
+        scratch_shapes=[pltpu.VMEM((STEP * TLEN, rows), F32), pltpu.VMEM((chans, rows), F32)],
         compiler_params=pltpu.CompilerParams(vmem_limit_bytes=26 * MIB),
         cost_estimate=pl.CostEstimate(flops=0, bytes_accessed=4 * rows * chans * TLEN, transcendentals=0),
     )(templates, valid)
@@ -214,10 +190,10 @@
     rows = w.shape[2]
     return pl.pallas_call(
         lambda *refs: slab_kernel(open_at, *refs),
-        in_specs=[VMEM, VMEM, VMEM, ANY],
+        in_specs=[VMEM] * 4,
         out_specs=[VMEM] * 2,
         out_shape=[jax.ShapeDtypeStruct((pieces // 2, rows // pieces, slab + 128), F32)] * 2,
-        scratch_shapes=[pltpu.VMEM((chans, EDGE), x.dtype)] + scratch(chans, slab, rows) + [pltpu.SemaphoreType.DMA],
+        scratch_shapes=scratch(chans, slab, rows),
         compiler_params=pltpu.CompilerParams(vmem_limit_bytes=18 * MIB),
         cost_estimate=pl.CostEstimate(flops=3 * rows * chans * TLEN * slab, bytes_accessed=2 * rows * chans * TLEN, transcendentals=0),
     )(w, norm, x, follows)

time: 77.1 us -> 75.5 us (0.979)
  Pallas kernels: 40.6 us -> 39 us
    pallas_call x5, Pallas kernels: 37.7 us -> 36.2 us  [the longest x3 31.2 us: correlated(): pl.pallas_call(lambda *refs: slab_kernel(open_at, *refs), in_specs=[VMEM]...]
  transfers between devices with their start and end apart: 15 -> 15, of which waited for: 5 -> 5; matrix products, arithmetic and copies ran while one was open for 0% -> 0% of each run, Pallas kernels for 52% -> 51%
where the time goes in v3:
time: 75.5 us; the launch traced here: 75.4 us
  Pallas kernels  39 us (52%)
  starting transfers between devices  19 us (25%)
  waiting for transfers between devices  14.5 us (19%)
  local copies, waits for them, and re-layouts  2.34 us (3%)
    pallas_call x3, Pallas kernels, correlated(): pl.pallas_call(lambda *refs: slab_kernel(open_at, *refs), in_specs=[VMEM]...  31.2 us
    ppermute x6, starting transfers between devices, sent(): lax.ppermute(block, 'tm', [(i, (i + slabs) % n) for i in range(n)])  11.4 us
    ppermute x6, waiting for transfers between devices, sent(): lax.ppermute(block, 'tm', [(i, (i + slabs) % n) for i in range(n)])  8.36 us
    pallas_call x1, Pallas kernels, tap_major(): pl.pallas_call(relayout_kernel, in_specs=[VMEM] * 2, out_specs=[VMEM] * 2...  3.64 us
    ppermute x2, starting transfers between devices, sent(): return lax.ppermute(block, ('tm', 'chan'), route)  3.26 us
    ppermute x2, waiting for transfers between devices, sent(): return lax.ppermute(block, ('tm', 'chan'), route)  3.22 us
    ppermute x6, waiting for transfers between devices, sent(): return lax.ppermute(block, 'chan', [(k, k ^ distance) for k in range(m)])  2.95 us
    ppermute x6, starting transfers between devices, sent(): return lax.ppermute(block, 'chan', [(k, k ^ distance) for k in range(m)])  2.73 us
  transfers between devices with their start and end apart: 15, of which 5 were waited for; matrix products, arithmetic and copies ran while one was open for 0% of the time, Pallas kernels for 51%

profile of v3, /device:TPU:0, one launch (start us, length us, event | category | flops | bytes accessed | tf_op | source)
XLA Modules:
  0.0 75.4 jit_solution(7163299958603692639)
XLA Ops:
  0.0 6.0 %collective-permute-start.1 = (s32[128,256]{1,0:T(8,128)}, s32[128,256]{1,0:T(8,128)S(1)}, u32[]{:S(2)}, u32[]{:S(2)}) collective-permute-start(s32[128,256]{1,0:T(8,128)} %v0_ref.1), channel_id=1, source_target_pairs={{0,28},{4,0},{8,4},{12,8},{16,12},{20,16},{24,20},{28,24},{1,29},{... | collective-permute-start | bytes 393224 | tf_op jit(solution)/shard_map/ppermute | solution.py:275
  6.4 1.1 %copy-done.2 = bf16[256,1280]{1,0:T(8,128)(2,1)S(1)} copy-done((bf16[256,1280]{1,0:T(8,128)(2,1)S(1)}, bf16[256,1280]{1,0:T(8,128)(2,1)}, u32[]{:S(2)}) %copy-start.2) | copy-done | bytes 655384
  7.6 1.6 %collective-permute-start = (bf16[256,128]{1,0:T(8,128)(2,1)S(1)}, bf16[256,128]{1,0:T(8,128)(2,1)S(1)}, u32[]{:S(2)}, u32[]{:S(2)}) collective-permute-start(bf16[256,128]{1,0:T(8,128)(2,1)S(1)} %shard_map.38), channel_id=1, source_target_pairs={{4,0},{8,4},{12,8},{16,12},{20,16},{24,20},{28,24},{5,1},{9,5},{13... | collective-permute-start | bytes 196616 | tf_op jit(solution)/shard_map/ppermute | solution.py:289
  9.1 1.2 %copy-done = bf16[128,25600]{1,0:T(8,128)(2,1)S(1)} copy-done((bf16[128,25600]{1,0:T(8,128)(2,1)S(1)}, bf16[128,25600]{1,0:T(8,128)(2,1)}, u32[]{:S(2)}) %copy-start) | copy-done | bytes 6553624
  10.4 3.6 %shard_map.37 = (bf16[103,256,128]{2,1,0:T(8,128)(2,1)S(1)}, f32[128,128]{1,0:T(8,128)S(1)}) custom-call(bf16[128,25600]{1,0:T(8,128)(2,1)S(1)} %copy-done, s32[128,256]{1,0:T(8,128)S(1)} %copy-done.1), custom_call_target="tpu_custom_call" | custom-call | bytes 13107200 | tf_op jit(solution)/shard_map/pallas_call | solution.py:177
  14.1 1.5 %collective-permute-start.4 = (bf16[256,1280]{1,0:T(8,128)(2,1)S(1)}, bf16[256,1280]{1,0:T(8,128)(2,1)S(1)}, u32[]{:S(2)}, u32[]{:S(2)}) collective-permute-start(bf16[256,1280]{1,0:T(8,128)(2,1)S(1)} %copy-done.3), channel_id=1, source_target_pairs={{0,4},{4,8},{8,12},{12,16},{16,20},{20,24},{24,28},{28,0},{1,5},{5... | collective-permute-start | bytes 1966088 | tf_op jit(solution)/shard_map/ppermute | solution.py:275
  15.6 1.5 %collective-permute-start.7 = (bf16[256,1280]{1,0:T(8,128)(2,1)S(1)}, bf16[256,1280]{1,0:T(8,128)(2,1)S(1)}, u32[]{:S(2)}, u32[]{:S(2)}) collective-permute-start(bf16[256,1280]{1,0:T(8,128)(2,1)S(1)} %copy-done.3), channel_id=1, source_target_pairs={{0,8},{4,12},{8,16},{12,20},{16,24},{20,28},{24,0},{28,4},{1,9},{5... | collective-permute-start | bytes 1966088 | tf_op jit(solution)/shard_map/ppermute | solution.py:275
  17.1 1.3 %shard_map.39 = (f32[2,3,32,1408]{3,2,1,0:T(8,128)S(1)}, f32[2,3,32,1408]{3,2,1,0:T(8,128)S(1)}) custom-call(bf16[256,1280]{1,0:T(8,128)(2,1)S(1)} %copy-done.3, bf16[256,128]{1,0:T(8,128)(2,1)S(1)} %collective-permute-done.h_ref.refs_3_, s32[128,256]{1,0:T(8,128)S(1)} %copy-done.1, s32[128,256]{1,0:T(8,128)S(1)} %collective-permute-done.1.v1_ref, ...), custom_call_target="tpu_custom_call" | custom-call | flops 503316480 | bytes 2621440 | tf_op jit(solution)/shard_map/pallas_call | solution.py:165
  18.5 10.4 %shard_map.40 = (f32[2,32,1408]{2,1,0:T(8,128)S(1)}, f32[2,32,1408]{2,1,0:T(8,128)S(1)}) custom-call(bf16[103,256,128]{2,1,0:T(8,128)(2,1)S(1)} %get-tuple-element.45.refs_0_, f32[128,128]{1,0:T(8,128)S(1)} %get-tuple-element.46.refs_1_, bf16[256,1280]{1,0:T(8,128)(2,1)S(1)} %copy-done.3, bf16[256,128]{1,0:T(8,128)(2,1)S(1)} %collective-permute-done.h_ref.refs_3_), custom_call_target="tpu_custom_call" | custom-call | flops 12582912000 | bytes 6553600 | tf_op jit(solution)/shard_map/pallas_call | solution.py:191
  28.9 5.6 %collective-permute-done.4.refs_2_.refs_3_ = bf16[256,1280]{1,0:T(8,128)(2,1)S(1)} collective-permute-done((bf16[256,1280]{1,0:T(8,128)(2,1)S(1)}, bf16[256,1280]{1,0:T(8,128)(2,1)S(1)}, u32[]{:S(2)}, u32[]{:S(2)}) %collective-permute-start.4) | collective-permute-done | bytes 655392 | tf_op jit(solution)/shard_map/ppermute | solution.py:275
  34.5 1.5 %collective-permute-start.6 = (f32[3,32,1408]{2,1,0:T(8,128)S(1)}, f32[3,32,1408]{2,1,0:T(8,128)S(1)}, u32[]{:S(2)}, u32[]{:S(2)}) collective-permute-start(f32[3,32,1408]{2,1,0:T(8,128)S(1)} %add_bitcast_fusion), channel_id=1, source_target_pairs={{0,2},{1,3},{2,0},{3,1},{4,6},{5,7},{6,4},{7,5},{8,10},{9,11},{10,... | collective-permute-start | bytes 1622024 | tf_op jit(solution)/shard_map/ppermute | solution.py:277
  36.0 10.5 %shard_map.41 = (f32[2,32,1408]{2,1,0:T(8,128)S(1)}, f32[2,32,1408]{2,1,0:T(8,128)S(1)}) custom-call(bf16[103,256,128]{2,1,0:T(8,128)(2,1)S(1)} %get-tuple-element.45.refs_0_, f32[128,128]{1,0:T(8,128)S(1)} %get-tuple-element.46.refs_1_, bf16[256,1280]{1,0:T(8,128)(2,1)S(1)} %collective-permute-done.4.refs_2_.refs_3_, bf16[256,1280]{1,0:T(8,128)(2,1)S(1)} %copy-done.3), custom_call_target="tpu_custom_call" | custom-call | flops 12582912000 | bytes 6553600 | tf_op jit(solution)/shard_map/pallas_call | solution.py:191
  46.6 0.6 collective-permute-start.8
  47.2 1.3 %collective-permute-done.8 = f32[2,32,1408]{2,1,0:T(8,128)S(1)} collective-permute-done((f32[2,32,1408]{2,1,0:T(8,128)S(1)}, f32[2,32,1408]{2,1,0:T(8,128)S(1)}, u32[]{:S(2)}, u32[]{:S(2)}) %collective-permute-start.8) | collective-permute-done | bytes 360480 | tf_op jit(solution)/shard_map/ppermute | solution.py:277
  48.5 1.2 %collective-permute-start.10 = (f32[32,1408]{1,0:T(8,128)S(1)}, f32[32,1408]{1,0:T(8,128)S(1)}, u32[]{:S(2)}, u32[]{:S(2)}) collective-permute-start(f32[32,1408]{1,0:T(8,128)S(1)} %get-tuple-element.65), channel_id=1, source_target_pairs={{0,30},{1,31},{2,28},{3,29},{4,2},{5,3},{6,0},{7,1},{8,6},{9,7},{1... | collective-permute-start | bytes 540680 | tf_op jit(solution)/shard_map/ppermute | solution.py:279
  50.2 1.4 %collective-permute-start.9 = (f32[32,1408]{1,0:T(8,128)S(1)}, f32[32,1408]{1,0:T(8,128)S(1)}, u32[]{:S(2)}, u32[]{:S(2)}) collective-permute-start(f32[32,1408]{1,0:T(8,128)S(1)} %get-tuple-element.64), channel_id=1, source_target_pairs={{0,28},{4,0},{8,4},{12,8},{16,12},{20,16},{24,20},{28,24},{1,29},{... | collective-permute-start | bytes 540680 | tf_op jit(solution)/shard_map/ppermute | solution.py:275
  51.6 10.3 %shard_map.42 = (f32[2,32,1408]{2,1,0:T(8,128)S(1)}, f32[2,32,1408]{2,1,0:T(8,128)S(1)}) custom-call(bf16[103,256,128]{2,1,0:T(8,128)(2,1)S(1)} %get-tuple-element.45.refs_0_, f32[128,128]{1,0:T(8,128)S(1)} %get-tuple-element.46.refs_1_, bf16[256,1280]{1,0:T(8,128)(2,1)S(1)} %collective-permute-done.7.refs_2_, ...), custom_call_target="tpu_custom_call" | custom-call | flops 12582912000 | bytes 6553600 | tf_op jit(solution)/shard_map/pallas_call | solution.py:191
  62.1 1.7 %collective-permute-done.12 = f32[2,32,1408]{2,1,0:T(8,128)S(1)} collective-permute-done((f32[2,32,1408]{2,1,0:T(8,128)S(1)}, f32[2,32,1408]{2,1,0:T(8,128)S(1)}, u32[]{:S(2)}, u32[]{:S(2)}) %collective-permute-start.12) | collective-permute-done | bytes 360480 | tf_op jit(solution)/shard_map/ppermute | solution.py:277
  63.8 0.6 collective-permute-start.13
  64.4 2.0 %collective-permute-start.14 = (f32[32,1408]{1,0:T(8,128)S(1)}, f32[32,1408]{1,0:T(8,128)S(1)}, u32[]{:S(2)}, u32[]{:S(2)}) collective-permute-start(f32[32,1408]{1,0:T(8,128)S(1)} %get-tuple-element.75), channel_id=1, source_target_pairs={{0,26},{1,27},{2,24},{3,25},{4,30},{5,31},{6,28},{7,29},{8,2},{9,3... | collective-permute-start | bytes 540680 | tf_op jit(solution)/shard_map/ppermute | solution.py:279
  66.4 2.0 %shard_map.43 = (f32[3,32,1280]{2,1,0:T(8,128)}, f32[32,1280]{1,0:T(8,128)S(1)}, f32[32,128]{1,0:T(8,128)S(1)}) custom-call(f32[2,3,32,1408]{3,2,1,0:T(8,128)S(1)} %get-tuple-element.44.refs_0_, f32[2,3,32,1408]{3,2,1,0:T(8,128)S(1)} %collective-permute-done.3.refs_1_, f32[3,32,1408]{2,1,0:T(8,128)S(1)} %collective-permute-done.6.refs_2_, ...), custom_call_target="tpu_custom_call" | custom-call | tf_op jit(solution)/shard_map/pallas_call | solution.py:243
  68.4 2.8 %collective-permute-done.13.refs_3_ = f32[32,1408]{1,0:T(8,128)S(1)} collective-permute-done((f32[32,1408]{1,0:T(8,128)S(1)}, f32[32,1408]{1,0:T(8,128)S(1)}, u32[]{:S(2)}, u32[]{:S(2)}) %collective-permute-start.13) | collective-permute-done | bytes 180256 | tf_op jit(solution)/shard_map/ppermute | solution.py:275
  71.2 3.2 %collective-permute-done.14.refs_4_ = f32[32,1408]{1,0:T(8,128)S(1)} collective-permute-done((f32[32,1408]{1,0:T(8,128)S(1)}, f32[32,1408]{1,0:T(8,128)S(1)}, u32[]{:S(2)}, u32[]{:S(2)}) %collective-permute-start.14) | collective-permute-done | bytes 180256 | tf_op jit(solution)/shard_map/ppermute | solution.py:279
  74.4 0.8 %shard_map.44 = f32[3,32,1280]{2,1,0:T(8,128)} custom-call(f32[3,32,1280]{2,1,0:T(8,128)} %get-tuple-element.70.refs_0_, f32[32,1280]{1,0:T(8,128)S(1)} %get-tuple-element.71.refs_1_, f32[32,128]{1,0:T(8,128)S(1)} %get-tuple-element.72.refs_2_, f32[32,1408]{1,0:T(8,128)S(1)} %collective-permute-done.13.refs_3_, ...), custom_call_target="tpu_custom_call", output_to_operand_aliasing={{}: (0, {})} | custom-call | tf_op jit(solution)/shard_map/pallas_call | solution.py:261
  (26 shorter events, 1.3 us)
Async XLA Ops:
  0.0 9.1 %copy-start.1 = (s32[128,256]{1,0:T(8,128)S(1)}, s32[128,256]{1,0:T(8,128)}, u32[]{:S(2)}) copy-start(s32[128,256]{1,0:T(8,128)} %v0_ref.1) | copy-start | bytes 393220
  0.0 14.0 %collective-permute-start.1 = (s32[128,256]{1,0:T(8,128)}, s32[128,256]{1,0:T(8,128)S(1)}, u32[]{:S(2)}, u32[]{:S(2)}) collective-permute-start(s32[128,256]{1,0:T(8,128)} %v0_ref.1), channel_id=1, source_target_pairs={{0,28},{4,0},{8,4},{12,8},{16,12},{20,16},{24,20},{28,24},{1,29},{... | collective-permute-start | bytes 393224 | tf_op jit(solution)/shard_map/ppermute | solution.py:275
  6.0 8.1 %collective-permute-start.2 = (s32[128,256]{1,0:T(8,128)}, s32[128,256]{1,0:T(8,128)S(1)}, u32[]{:S(2)}, u32[]{:S(2)}) collective-permute-start(s32[128,256]{1,0:T(8,128)} %v0_ref.1), channel_id=1, source_target_pairs={{0,24},{4,28},{8,0},{12,4},{16,8},{20,12},{24,16},{28,20},{1,25},{... | collective-permute-start | bytes 393224 | tf_op jit(solution)/shard_map/ppermute | solution.py:275
  6.4 1.1 %copy-start.2 = (bf16[256,1280]{1,0:T(8,128)(2,1)S(1)}, bf16[256,1280]{1,0:T(8,128)(2,1)}, u32[]{:S(2)}) copy-start(bf16[256,1280]{1,0:T(8,128)(2,1)} %refs_3_.1) | copy-start | bytes 1966084
  7.5 2.9 %copy-start = (bf16[128,25600]{1,0:T(8,128)(2,1)S(1)}, bf16[128,25600]{1,0:T(8,128)(2,1)}, u32[]{:S(2)}) copy-start(bf16[128,25600]{1,0:T(8,128)(2,1)} %t_ref.1) | copy-start | bytes 19660804
  7.5 6.5 %copy-start.3 = (bf16[256,1280]{1,0:T(8,128)(2,1)S(1)}, bf16[256,1280]{1,0:T(8,128)(2,1)}, u32[]{:S(2)}) copy-start(bf16[256,1280]{1,0:T(8,128)(2,1)} %refs_3_.1) | copy-start | bytes 1966084
  7.6 6.5 %collective-permute-start = (bf16[256,128]{1,0:T(8,128)(2,1)S(1)}, bf16[256,128]{1,0:T(8,128)(2,1)S(1)}, u32[]{:S(2)}, u32[]{:S(2)}) collective-permute-start(bf16[256,128]{1,0:T(8,128)(2,1)S(1)} %shard_map.38), channel_id=1, source_target_pairs={{4,0},{8,4},{12,8},{16,12},{20,16},{24,20},{28,24},{5,1},{9,5},{13... | collective-permute-start | bytes 196616 | tf_op jit(solution)/shard_map/ppermute | solution.py:289
  14.1 20.4 %collective-permute-start.4 = (bf16[256,1280]{1,0:T(8,128)(2,1)S(1)}, bf16[256,1280]{1,0:T(8,128)(2,1)S(1)}, u32[]{:S(2)}, u32[]{:S(2)}) collective-permute-start(bf16[256,1280]{1,0:T(8,128)(2,1)S(1)} %copy-done.3), channel_id=1, source_target_pairs={{0,4},{4,8},{8,12},{12,16},{16,20},{20,24},{24,28},{28,0},{1,5},{5... | collective-permute-start | bytes 1966088 | tf_op jit(solution)/shard_map/ppermute | solution.py:275
  15.6 32.9 %collective-permute-start.7 = (bf16[256,1280]{1,0:T(8,128)(2,1)S(1)}, bf16[256,1280]{1,0:T(8,128)(2,1)S(1)}, u32[]{:S(2)}, u32[]{:S(2)}) collective-permute-start(bf16[256,1280]{1,0:T(8,128)(2,1)S(1)} %copy-done.3), channel_id=1, source_target_pairs={{0,8},{4,12},{8,16},{12,20},{16,24},{20,28},{24,0},{28,4},{1,9},{5... | collective-permute-start | bytes 1966088 | tf_op jit(solution)/shard_map/ppermute | solution.py:275
  18.4 10.4 %collective-permute-start.3 = (f32[2,3,32,1408]{3,2,1,0:T(8,128)S(1)}, f32[2,3,32,1408]{3,2,1,0:T(8,128)S(1)}, u32[]{:S(2)}, u32[]{:S(2)}) collective-permute-start(f32[2,3,32,1408]{3,2,1,0:T(8,128)S(1)} %get-tuple-element.50), channel_id=1, source_target_pairs={{0,1},{1,0},{2,3},{3,2},{4,5},{5,4},{6,7},{7,6},{8,9},{9,8},{10,11... | collective-permute-start | bytes 3244040 | tf_op jit(solution)/shard_map/ppermute | solution.py:277
  34.5 12.1 %collective-permute-start.6 = (f32[3,32,1408]{2,1,0:T(8,128)S(1)}, f32[3,32,1408]{2,1,0:T(8,128)S(1)}, u32[]{:S(2)}, u32[]{:S(2)}) collective-permute-start(f32[3,32,1408]{2,1,0:T(8,128)S(1)} %add_bitcast_fusion), channel_id=1, source_target_pairs={{0,2},{1,3},{2,0},{3,1},{4,6},{5,7},{6,4},{7,5},{8,10},{9,11},{10,... | collective-permute-start | bytes 1622024 | tf_op jit(solution)/shard_map/ppermute | solution.py:277
  36.0 10.6 %collective-permute-start.5 = (f32[2,32,1408]{2,1,0:T(8,128)S(1)}, f32[2,32,1408]{2,1,0:T(8,128)S(1)}, u32[]{:S(2)}, u32[]{:S(2)}) collective-permute-start(f32[2,32,1408]{2,1,0:T(8,128)S(1)} %get-tuple-element.55), channel_id=1, source_target_pairs={{0,1},{1,0},{2,3},{3,2},{4,5},{5,4},{6,7},{7,6},{8,9},{9,8},{10,11... | collective-permute-start | bytes 1081352 | tf_op jit(solution)/shard_map/ppermute | solution.py:277
  46.6 1.9 %collective-permute-start.8 = (f32[2,32,1408]{2,1,0:T(8,128)S(1)}, f32[2,32,1408]{2,1,0:T(8,128)S(1)}, u32[]{:S(2)}, u32[]{:S(2)}) collective-permute-start(f32[2,32,1408]{2,1,0:T(8,128)S(1)} %get-tuple-element.61), channel_id=1, source_target_pairs={{0,1},{1,0},{2,3},{3,2},{4,5},{5,4},{6,7},{7,6},{8,9},{9,8},{10,11... | collective-permute-start | bytes 1081352 | tf_op jit(solution)/shard_map/ppermute | solution.py:277
  48.5 13.5 %collective-permute-start.10 = (f32[32,1408]{1,0:T(8,128)S(1)}, f32[32,1408]{1,0:T(8,128)S(1)}, u32[]{:S(2)}, u32[]{:S(2)}) collective-permute-start(f32[32,1408]{1,0:T(8,128)S(1)} %get-tuple-element.65), channel_id=1, source_target_pairs={{0,30},{1,31},{2,28},{3,29},{4,2},{5,3},{6,0},{7,1},{8,6},{9,7},{1... | collective-permute-start | bytes 540680 | tf_op jit(solution)/shard_map/ppermute | solution.py:279
  49.7 12.2 %collective-permute-start.11 = (f32[32,1408]{1,0:T(8,128)S(1)}, f32[32,1408]{1,0:T(8,128)S(1)}, u32[]{:S(2)}, u32[]{:S(2)}) collective-permute-start(f32[32,1408]{1,0:T(8,128)S(1)} %add_bitcast_fusion.1), channel_id=1, source_target_pairs={{0,2},{1,3},{2,0},{3,1},{4,6},{5,7},{6,4},{7,5},{8,10},{9,11},{10,... | collective-permute-start | bytes 540680 | tf_op jit(solution)/shard_map/ppermute | solution.py:277
  50.2 11.8 %collective-permute-start.9 = (f32[32,1408]{1,0:T(8,128)S(1)}, f32[32,1408]{1,0:T(8,128)S(1)}, u32[]{:S(2)}, u32[]{:S(2)}) collective-permute-start(f32[32,1408]{1,0:T(8,128)S(1)} %get-tuple-element.64), channel_id=1, source_target_pairs={{0,28},{4,0},{8,4},{12,8},{16,12},{20,16},{24,20},{28,24},{1,29},{... | collective-permute-start | bytes 540680 | tf_op jit(solution)/shard_map/ppermute | solution.py:275
  62.0 1.7 %collective-permute-start.12 = (f32[2,32,1408]{2,1,0:T(8,128)S(1)}, f32[2,32,1408]{2,1,0:T(8,128)S(1)}, u32[]{:S(2)}, u32[]{:S(2)}) collective-permute-start(f32[2,32,1408]{2,1,0:T(8,128)S(1)} %get-tuple-element.74), channel_id=1, source_target_pairs={{0,1},{1,0},{2,3},{3,2},{4,5},{5,4},{6,7},{7,6},{8,9},{9,8},{10,11... | collective-permute-start | bytes 1081352 | tf_op jit(solution)/shard_map/ppermute | solution.py:277
  63.8 7.4 %collective-permute-start.13 = (f32[32,1408]{1,0:T(8,128)S(1)}, f32[32,1408]{1,0:T(8,128)S(1)}, u32[]{:S(2)}, u32[]{:S(2)}) collective-permute-start(f32[32,1408]{1,0:T(8,128)S(1)} %get-tuple-element.76), channel_id=1, source_target_pairs={{0,24},{4,28},{8,0},{12,4},{16,8},{20,12},{24,16},{28,20},{1,25},{... | collective-permute-start | bytes 540680 | tf_op jit(solution)/shard_map/ppermute | solution.py:275
  64.4 10.1 %collective-permute-start.14 = (f32[32,1408]{1,0:T(8,128)S(1)}, f32[32,1408]{1,0:T(8,128)S(1)}, u32[]{:S(2)}, u32[]{:S(2)}) collective-permute-start(f32[32,1408]{1,0:T(8,128)S(1)} %get-tuple-element.75), channel_id=1, source_target_pairs={{0,26},{1,27},{2,24},{3,25},{4,30},{5,31},{6,28},{7,29},{8,2},{9,3... | collective-permute-start | bytes 540680 | tf_op jit(solution)/shard_map/ppermute | solution.py:279

commit v4 on v3

--- a/solution.py
+++ b/solution.py
@@ -302,7 +302,7 @@
     give0, power_got = together((give0, power_got))
     got0 = sent(give0, 0, 1)
     powers = [power_keep[d] + power_got[d] for d in others]
-    earlier, powers = together((earlier, powers))
+    earlier, _ = together((earlier, powers))
     powers = [sent(part, 0, 2 * d) for d, part in zip(others, powers)]
 
     keep1, give1 = correlated(w, norm, earlier, data, 0, pieces)
@@ -310,7 +310,7 @@
     got1 = sent(give1, 0, 1)
     num0 = [keep0[d] + got0[d] for d in others]
     num1 = [keep1[d] + got1[d] for d in range(pieces // 2)]
-    earliest, num0, num1 = together((earliest, num0, num1))
+    earliest, _, _ = together((earliest, num0, num1))
     num0 = [sent(part, 0, 2 * d) for d, part in zip(others, num0)]
     num1 = [sent(part, -1, 2 * d) for d, part in enumerate(num1)]
 

time: 75.5 us -> 73.9 us (0.979)
  waiting for transfers between devices: 14.5 us -> 11.8 us
  starting transfers between devices: 19 us -> 20.1 us
    ppermute x6, starting transfers between devices: 11.4 us -> 9.98 us  [sent(): lax.ppermute(block, 'tm', [(i, (i + slabs) % n) for i in range(n)])]
    ppermute x2, starting transfers between devices: 3.26 us -> 4.64 us  [sent(): return lax.ppermute(block, ('tm', 'chan'), route)]
    ppermute x6, waiting for transfers between devices: 2.95 us -> 1.68 us  [sent(): return lax.ppermute(block, 'chan', [(k, k ^ distance) for k in range(m)])]
    ppermute x6, waiting for transfers between devices: 8.36 us -> 7.1 us  [sent(): lax.ppermute(block, 'tm', [(i, (i + slabs) % n) for i in range(n)])]
    ppermute x6, starting transfers between devices: 2.73 us -> 3.91 us  [sent(): return lax.ppermute(block, 'chan', [(k, k ^ distance) for k in range(m)])]
  transfers between devices with their start and end apart: 15 -> 15, of which waited for: 5 -> 4; matrix products, arithmetic and copies ran while one was open for 0% -> 0% of each run, Pallas kernels for 51% -> 52%
where the time goes in v4:
time: 73.9 us; the launch traced here: 73.7 us
  Pallas kernels  39 us (53%)
  starting transfers between devices  20.1 us (27%)
  waiting for transfers between devices  11.8 us (16%)
  local copies, waits for them, and re-layouts  2.34 us (3%)
    pallas_call x3, Pallas kernels, correlated(): pl.pallas_call(lambda *refs: slab_kernel(open_at, *refs), in_specs=[VMEM]...  31.2 us
    ppermute x6, starting transfers between devices, sent(): lax.ppermute(block, 'tm', [(i, (i + slabs) % n) for i in range(n)])  9.98 us
    ppermute x6, waiting for transfers between devices, sent(): lax.ppermute(block, 'tm', [(i, (i + slabs) % n) for i in range(n)])  7.1 us
    ppermute x2, starting transfers between devices, sent(): return lax.ppermute(block, ('tm', 'chan'), route)  4.64 us
    ppermute x6, starting transfers between devices, sent(): return lax.ppermute(block, 'chan', [(k, k ^ distance) for k in range(m)])  3.91 us
    pallas_call x1, Pallas kernels, tap_major(): pl.pallas_call(relayout_kernel, in_specs=[VMEM] * 2, out_specs=[VMEM] * 2...  3.64 us
    ppermute x2, waiting for transfers between devices, sent(): return lax.ppermute(block, ('tm', 'chan'), route)  2.99 us
    unnamed x8, local copies, waits for them, and re-layouts  2.34 us
  transfers between devices with their start and end apart: 15, of which 4 were waited for; matrix products, arithmetic and copies ran while one was open for 0% of the time, Pallas kernels for 52%

profile of v4, /device:TPU:0, one launch (start us, length us, event | category | flops | bytes accessed | tf_op | source)
XLA Modules:
  0.0 73.7 jit_solution(18088303977204848432)
XLA Ops:
  0.0 6.0 %collective-permute-start.1 = (s32[128,256]{1,0:T(8,128)}, s32[128,256]{1,0:T(8,128)S(1)}, u32[]{:S(2)}, u32[]{:S(2)}) collective-permute-start(s32[128,256]{1,0:T(8,128)} %v0_ref.1), channel_id=1, source_target_pairs={{0,28},{4,0},{8,4},{12,8},{16,12},{20,16},{24,20},{28,24},{1,29},{... | collective-permute-start | bytes 393224 | tf_op jit(solution)/shard_map/ppermute | solution.py:275
  6.0 0.4 collective-permute-start.2
  6.4 1.1 %copy-done.2 = bf16[256,1280]{1,0:T(8,128)(2,1)S(1)} copy-done((bf16[256,1280]{1,0:T(8,128)(2,1)S(1)}, bf16[256,1280]{1,0:T(8,128)(2,1)}, u32[]{:S(2)}) %copy-start.2) | copy-done | bytes 655384
  7.6 1.6 %collective-permute-start = (bf16[256,128]{1,0:T(8,128)(2,1)S(1)}, bf16[256,128]{1,0:T(8,128)(2,1)S(1)}, u32[]{:S(2)}, u32[]{:S(2)}) collective-permute-start(bf16[256,128]{1,0:T(8,128)(2,1)S(1)} %shard_map.38), channel_id=1, source_target_pairs={{4,0},{8,4},{12,8},{16,12},{20,16},{24,20},{28,24},{5,1},{9,5},{13... | collective-permute-start | bytes 196616 | tf_op jit(solution)/shard_map/ppermute | solution.py:289
  9.1 1.2 %copy-done = bf16[128,25600]{1,0:T(8,128)(2,1)S(1)} copy-done((bf16[128,25600]{1,0:T(8,128)(2,1)S(1)}, bf16[128,25600]{1,0:T(8,128)(2,1)}, u32[]{:S(2)}) %copy-start) | copy-done | bytes 6553624
  10.4 3.6 %shard_map.37 = (bf16[103,256,128]{2,1,0:T(8,128)(2,1)S(1)}, f32[128,128]{1,0:T(8,128)S(1)}) custom-call(bf16[128,25600]{1,0:T(8,128)(2,1)S(1)} %copy-done, s32[128,256]{1,0:T(8,128)S(1)} %copy-done.1), custom_call_target="tpu_custom_call" | custom-call | bytes 13107200 | tf_op jit(solution)/shard_map/pallas_call | solution.py:177
  14.1 1.5 %collective-permute-start.4 = (bf16[256,1280]{1,0:T(8,128)(2,1)S(1)}, bf16[256,1280]{1,0:T(8,128)(2,1)S(1)}, u32[]{:S(2)}, u32[]{:S(2)}) collective-permute-start(bf16[256,1280]{1,0:T(8,128)(2,1)S(1)} %copy-done.3), channel_id=1, source_target_pairs={{0,4},{4,8},{8,12},{12,16},{16,20},{20,24},{24,28},{28,0},{1,5},{5... | collective-permute-start | bytes 1966088 | tf_op jit(solution)/shard_map/ppermute | solution.py:275
  15.6 1.5 %collective-permute-start.7 = (bf16[256,1280]{1,0:T(8,128)(2,1)S(1)}, bf16[256,1280]{1,0:T(8,128)(2,1)S(1)}, u32[]{:S(2)}, u32[]{:S(2)}) collective-permute-start(bf16[256,1280]{1,0:T(8,128)(2,1)S(1)} %copy-done.3), channel_id=1, source_target_pairs={{0,8},{4,12},{8,16},{12,20},{16,24},{20,28},{24,0},{28,4},{1,9},{5... | collective-permute-start | bytes 1966088 | tf_op jit(solution)/shard_map/ppermute | solution.py:275
  17.1 1.3 %shard_map.39 = (f32[2,3,32,1408]{3,2,1,0:T(8,128)S(1)}, f32[2,3,32,1408]{3,2,1,0:T(8,128)S(1)}) custom-call(bf16[256,1280]{1,0:T(8,128)(2,1)S(1)} %copy-done.3, bf16[256,128]{1,0:T(8,128)(2,1)S(1)} %collective-permute-done.h_ref.refs_3_, s32[128,256]{1,0:T(8,128)S(1)} %copy-done.1, s32[128,256]{1,0:T(8,128)S(1)} %collective-permute-done.1.v1_ref, ...), custom_call_target="tpu_custom_call" | custom-call | flops 503316480 | bytes 2621440 | tf_op jit(solution)/shard_map/pallas_call | solution.py:165
  18.5 10.4 %shard_map.40 = (f32[2,32,1408]{2,1,0:T(8,128)S(1)}, f32[2,32,1408]{2,1,0:T(8,128)S(1)}) custom-call(bf16[103,256,128]{2,1,0:T(8,128)(2,1)S(1)} %get-tuple-element.41.refs_0_, f32[128,128]{1,0:T(8,128)S(1)} %get-tuple-element.42.refs_1_, bf16[256,1280]{1,0:T(8,128)(2,1)S(1)} %copy-done.3, bf16[256,128]{1,0:T(8,128)(2,1)S(1)} %collective-permute-done.h_ref.refs_3_), custom_call_target="tpu_custom_call" | custom-call | flops 12582912000 | bytes 6553600 | tf_op jit(solution)/shard_map/pallas_call | solution.py:191
  28.9 1.6 %collective-permute-start.6 = (f32[3,32,1408]{2,1,0:T(8,128)S(1)}, f32[3,32,1408]{2,1,0:T(8,128)S(1)}, u32[]{:S(2)}, u32[]{:S(2)}) collective-permute-start(f32[3,32,1408]{2,1,0:T(8,128)S(1)} %add_bitcast_fusion), channel_id=1, source_target_pairs={{0,2},{1,3},{2,0},{3,1},{4,6},{5,7},{6,4},{7,5},{8,10},{9,11},{10,... | collective-permute-start | bytes 1622024 | tf_op jit(solution)/shard_map/ppermute | solution.py:277
  30.5 4.0 %collective-permute-done.4.refs_2_.refs_3_ = bf16[256,1280]{1,0:T(8,128)(2,1)S(1)} collective-permute-done((bf16[256,1280]{1,0:T(8,128)(2,1)S(1)}, bf16[256,1280]{1,0:T(8,128)(2,1)S(1)}, u32[]{:S(2)}, u32[]{:S(2)}) %collective-permute-start.4) | collective-permute-done | bytes 655392 | tf_op jit(solution)/shard_map/ppermute | solution.py:275
  34.5 10.5 %shard_map.41 = (f32[2,32,1408]{2,1,0:T(8,128)S(1)}, f32[2,32,1408]{2,1,0:T(8,128)S(1)}) custom-call(bf16[103,256,128]{2,1,0:T(8,128)(2,1)S(1)} %get-tuple-element.41.refs_0_, f32[128,128]{1,0:T(8,128)S(1)} %get-tuple-element.42.refs_1_, bf16[256,1280]{1,0:T(8,128)(2,1)S(1)} %collective-permute-done.4.refs_2_.refs_3_, bf16[256,1280]{1,0:T(8,128)(2,1)S(1)} %copy-done.3), custom_call_target="tpu_custom_call" | custom-call | flops 12582912000 | bytes 6553600 | tf_op jit(solution)/shard_map/pallas_call | solution.py:191
  45.1 0.6 collective-permute-start.8
  45.7 1.6 %collective-permute-start.11 = (f32[32,1408]{1,0:T(8,128)S(1)}, f32[32,1408]{1,0:T(8,128)S(1)}, u32[]{:S(2)}, u32[]{:S(2)}) collective-permute-start(f32[32,1408]{1,0:T(8,128)S(1)} %add_bitcast_fusion.1), channel_id=1, source_target_pairs={{0,2},{1,3},{2,0},{3,1},{4,6},{5,7},{6,4},{7,5},{8,10},{9,11},{10,... | collective-permute-start | bytes 540680 | tf_op jit(solution)/shard_map/ppermute | solution.py:277
  47.3 2.4 %collective-permute-start.10 = (f32[32,1408]{1,0:T(8,128)S(1)}, f32[32,1408]{1,0:T(8,128)S(1)}, u32[]{:S(2)}, u32[]{:S(2)}) collective-permute-start(f32[32,1408]{1,0:T(8,128)S(1)} %get-tuple-element.69), channel_id=1, source_target_pairs={{0,30},{1,31},{2,28},{3,29},{4,2},{5,3},{6,0},{7,1},{8,6},{9,7},{1... | collective-permute-start | bytes 540680 | tf_op jit(solution)/shard_map/ppermute | solution.py:279
  49.7 0.5 collective-permute-start.9
  50.2 10.3 %shard_map.42 = (f32[2,32,1408]{2,1,0:T(8,128)S(1)}, f32[2,32,1408]{2,1,0:T(8,128)S(1)}) custom-call(bf16[103,256,128]{2,1,0:T(8,128)(2,1)S(1)} %get-tuple-element.41.refs_0_, f32[128,128]{1,0:T(8,128)S(1)} %get-tuple-element.42.refs_1_, bf16[256,1280]{1,0:T(8,128)(2,1)S(1)} %collective-permute-done.7.refs_2_, ...), custom_call_target="tpu_custom_call" | custom-call | flops 12582912000 | bytes 6553600 | tf_op jit(solution)/shard_map/pallas_call | solution.py:191
  60.7 1.7 %collective-permute-done.12 = f32[2,32,1408]{2,1,0:T(8,128)S(1)} collective-permute-done((f32[2,32,1408]{2,1,0:T(8,128)S(1)}, f32[2,32,1408]{2,1,0:T(8,128)S(1)}, u32[]{:S(2)}, u32[]{:S(2)}) %collective-permute-start.12) | collective-permute-done | bytes 360480 | tf_op jit(solution)/shard_map/ppermute | solution.py:277
  62.4 2.2 %collective-permute-start.14 = (f32[32,1408]{1,0:T(8,128)S(1)}, f32[32,1408]{1,0:T(8,128)S(1)}, u32[]{:S(2)}, u32[]{:S(2)}) collective-permute-start(f32[32,1408]{1,0:T(8,128)S(1)} %get-tuple-element.67), channel_id=1, source_target_pairs={{0,26},{1,27},{2,24},{3,25},{4,30},{5,31},{6,28},{7,29},{8,2},{9,3... | collective-permute-start | bytes 540680 | tf_op jit(solution)/shard_map/ppermute | solution.py:279
  64.7 2.0 %shard_map.43 = (f32[3,32,1280]{2,1,0:T(8,128)}, f32[32,1280]{1,0:T(8,128)S(1)}, f32[32,128]{1,0:T(8,128)S(1)}) custom-call(f32[2,3,32,1408]{3,2,1,0:T(8,128)S(1)} %get-tuple-element.40.refs_0_, f32[2,3,32,1408]{3,2,1,0:T(8,128)S(1)} %collective-permute-done.3.refs_1_, f32[3,32,1408]{2,1,0:T(8,128)S(1)} %collective-permute-done.6.refs_2_, ...), custom_call_target="tpu_custom_call" | custom-call | tf_op jit(solution)/shard_map/pallas_call | solution.py:243
  66.7 3.1 %collective-permute-done.13.refs_3_ = f32[32,1408]{1,0:T(8,128)S(1)} collective-permute-done((f32[32,1408]{1,0:T(8,128)S(1)}, f32[32,1408]{1,0:T(8,128)S(1)}, u32[]{:S(2)}, u32[]{:S(2)}) %collective-permute-start.13) | collective-permute-done | bytes 180256 | tf_op jit(solution)/shard_map/ppermute | solution.py:275
  69.8 3.0 %collective-permute-done.14.refs_4_ = f32[32,1408]{1,0:T(8,128)S(1)} collective-permute-done((f32[32,1408]{1,0:T(8,128)S(1)}, f32[32,1408]{1,0:T(8,128)S(1)}, u32[]{:S(2)}, u32[]{:S(2)}) %collective-permute-start.14) | collective-permute-done | bytes 180256 | tf_op jit(solution)/shard_map/ppermute | solution.py:279
  72.8 0.8 %shard_map.44 = f32[3,32,1280]{2,1,0:T(8,128)} custom-call(f32[3,32,1280]{2,1,0:T(8,128)} %get-tuple-element.62.refs_0_, f32[32,1280]{1,0:T(8,128)S(1)} %get-tuple-element.63.refs_1_, f32[32,128]{1,0:T(8,128)S(1)} %get-tuple-element.64.refs_2_, f32[32,1408]{1,0:T(8,128)S(1)} %collective-permute-done.13.refs_3_, ...), custom_call_target="tpu_custom_call", output_to_operand_aliasing={{}: (0, {})} | custom-call | tf_op jit(solution)/shard_map/pallas_call | solution.py:261
  (26 shorter events, 0.4 us)
Async XLA Ops:
  0.0 9.1 %copy-start.1 = (s32[128,256]{1,0:T(8,128)S(1)}, s32[128,256]{1,0:T(8,128)}, u32[]{:S(2)}) copy-start(s32[128,256]{1,0:T(8,128)} %v0_ref.1) | copy-start | bytes 393220
  0.0 14.0 %collective-permute-start.1 = (s32[128,256]{1,0:T(8,128)}, s32[128,256]{1,0:T(8,128)S(1)}, u32[]{:S(2)}, u32[]{:S(2)}) collective-permute-start(s32[128,256]{1,0:T(8,128)} %v0_ref.1), channel_id=1, source_target_pairs={{0,28},{4,0},{8,4},{12,8},{16,12},{20,16},{24,20},{28,24},{1,29},{... | collective-permute-start | bytes 393224 | tf_op jit(solution)/shard_map/ppermute | solution.py:275
  6.0 8.1 %collective-permute-start.2 = (s32[128,256]{1,0:T(8,128)}, s32[128,256]{1,0:T(8,128)S(1)}, u32[]{:S(2)}, u32[]{:S(2)}) collective-permute-start(s32[128,256]{1,0:T(8,128)} %v0_ref.1), channel_id=1, source_target_pairs={{0,24},{4,28},{8,0},{12,4},{16,8},{20,12},{24,16},{28,20},{1,25},{... | collective-permute-start | bytes 393224 | tf_op jit(solution)/shard_map/ppermute | solution.py:275
  6.4 1.1 %copy-start.2 = (bf16[256,1280]{1,0:T(8,128)(2,1)S(1)}, bf16[256,1280]{1,0:T(8,128)(2,1)}, u32[]{:S(2)}) copy-start(bf16[256,1280]{1,0:T(8,128)(2,1)} %refs_3_.1) | copy-start | bytes 1966084
  7.5 2.9 %copy-start = (bf16[128,25600]{1,0:T(8,128)(2,1)S(1)}, bf16[128,25600]{1,0:T(8,128)(2,1)}, u32[]{:S(2)}) copy-start(bf16[128,25600]{1,0:T(8,128)(2,1)} %t_ref.1) | copy-start | bytes 19660804
  7.5 6.5 %copy-start.3 = (bf16[256,1280]{1,0:T(8,128)(2,1)S(1)}, bf16[256,1280]{1,0:T(8,128)(2,1)}, u32[]{:S(2)}) copy-start(bf16[256,1280]{1,0:T(8,128)(2,1)} %refs_3_.1) | copy-start | bytes 1966084
  7.6 6.5 %collective-permute-start = (bf16[256,128]{1,0:T(8,128)(2,1)S(1)}, bf16[256,128]{1,0:T(8,128)(2,1)S(1)}, u32[]{:S(2)}, u32[]{:S(2)}) collective-permute-start(bf16[256,128]{1,0:T(8,128)(2,1)S(1)} %shard_map.38), channel_id=1, source_target_pairs={{4,0},{8,4},{12,8},{16,12},{20,16},{24,20},{28,24},{5,1},{9,5},{13... | collective-permute-start | bytes 196616 | tf_op jit(solution)/shard_map/ppermute | solution.py:289
  14.1 20.4 %collective-permute-start.4 = (bf16[256,1280]{1,0:T(8,128)(2,1)S(1)}, bf16[256,1280]{1,0:T(8,128)(2,1)S(1)}, u32[]{:S(2)}, u32[]{:S(2)}) collective-permute-start(bf16[256,1280]{1,0:T(8,128)(2,1)S(1)} %copy-done.3), channel_id=1, source_target_pairs={{0,4},{4,8},{8,12},{12,16},{16,20},{20,24},{24,28},{28,0},{1,5},{5... | collective-permute-start | bytes 1966088 | tf_op jit(solution)/shard_map/ppermute | solution.py:275
  15.6 34.6 %collective-permute-start.7 = (bf16[256,1280]{1,0:T(8,128)(2,1)S(1)}, bf16[256,1280]{1,0:T(8,128)(2,1)S(1)}, u32[]{:S(2)}, u32[]{:S(2)}) collective-permute-start(bf16[256,1280]{1,0:T(8,128)(2,1)S(1)} %copy-done.3), channel_id=1, source_target_pairs={{0,8},{4,12},{8,16},{12,20},{16,24},{20,28},{24,0},{28,4},{1,9},{5... | collective-permute-start | bytes 1966088 | tf_op jit(solution)/shard_map/ppermute | solution.py:275
  18.4 10.4 %collective-permute-start.3 = (f32[2,3,32,1408]{3,2,1,0:T(8,128)S(1)}, f32[2,3,32,1408]{3,2,1,0:T(8,128)S(1)}, u32[]{:S(2)}, u32[]{:S(2)}) collective-permute-start(f32[2,3,32,1408]{3,2,1,0:T(8,128)S(1)} %get-tuple-element.46), channel_id=1, source_target_pairs={{0,1},{1,0},{2,3},{3,2},{4,5},{5,4},{6,7},{7,6},{8,9},{9,8},{10,11... | collective-permute-start | bytes 3244040 | tf_op jit(solution)/shard_map/ppermute | solution.py:277
  28.9 16.1 %collective-permute-start.6 = (f32[3,32,1408]{2,1,0:T(8,128)S(1)}, f32[3,32,1408]{2,1,0:T(8,128)S(1)}, u32[]{:S(2)}, u32[]{:S(2)}) collective-permute-start(f32[3,32,1408]{2,1,0:T(8,128)S(1)} %add_bitcast_fusion), channel_id=1, source_target_pairs={{0,2},{1,3},{2,0},{3,1},{4,6},{5,7},{6,4},{7,5},{8,10},{9,11},{10,... | collective-permute-start | bytes 1622024 | tf_op jit(solution)/shard_map/ppermute | solution.py:277
  34.5 10.5 %collective-permute-start.5 = (f32[2,32,1408]{2,1,0:T(8,128)S(1)}, f32[2,32,1408]{2,1,0:T(8,128)S(1)}, u32[]{:S(2)}, u32[]{:S(2)}) collective-permute-start(f32[2,32,1408]{2,1,0:T(8,128)S(1)} %get-tuple-element.51), channel_id=1, source_target_pairs={{0,1},{1,0},{2,3},{3,2},{4,5},{5,4},{6,7},{7,6},{8,9},{9,8},{10,11... | collective-permute-start | bytes 1081352 | tf_op jit(solution)/shard_map/ppermute | solution.py:277
  45.1 2.2 %collective-permute-start.8 = (f32[2,32,1408]{2,1,0:T(8,128)S(1)}, f32[2,32,1408]{2,1,0:T(8,128)S(1)}, u32[]{:S(2)}, u32[]{:S(2)}) collective-permute-start(f32[2,32,1408]{2,1,0:T(8,128)S(1)} %get-tuple-element.56), channel_id=1, source_target_pairs={{0,1},{1,0},{2,3},{3,2},{4,5},{5,4},{6,7},{7,6},{8,9},{9,8},{10,11... | collective-permute-start | bytes 1081352 | tf_op jit(solution)/shard_map/ppermute | solution.py:277
  45.7 14.9 %collective-permute-start.11 = (f32[32,1408]{1,0:T(8,128)S(1)}, f32[32,1408]{1,0:T(8,128)S(1)}, u32[]{:S(2)}, u32[]{:S(2)}) collective-permute-start(f32[32,1408]{1,0:T(8,128)S(1)} %add_bitcast_fusion.1), channel_id=1, source_target_pairs={{0,2},{1,3},{2,0},{3,1},{4,6},{5,7},{6,4},{7,5},{8,10},{9,11},{10,... | collective-permute-start | bytes 540680 | tf_op jit(solution)/shard_map/ppermute | solution.py:277
  47.3 13.2 %collective-permute-start.10 = (f32[32,1408]{1,0:T(8,128)S(1)}, f32[32,1408]{1,0:T(8,128)S(1)}, u32[]{:S(2)}, u32[]{:S(2)}) collective-permute-start(f32[32,1408]{1,0:T(8,128)S(1)} %get-tuple-element.69), channel_id=1, source_target_pairs={{0,30},{1,31},{2,28},{3,29},{4,2},{5,3},{6,0},{7,1},{8,6},{9,7},{1... | collective-permute-start | bytes 540680 | tf_op jit(solution)/shard_map/ppermute | solution.py:279
  49.7 10.8 %collective-permute-start.9 = (f32[32,1408]{1,0:T(8,128)S(1)}, f32[32,1408]{1,0:T(8,128)S(1)}, u32[]{:S(2)}, u32[]{:S(2)}) collective-permute-start(f32[32,1408]{1,0:T(8,128)S(1)} %get-tuple-element.70), channel_id=1, source_target_pairs={{0,28},{4,0},{8,4},{12,8},{16,12},{20,16},{24,20},{28,24},{1,29},{... | collective-permute-start | bytes 540680 | tf_op jit(solution)/shard_map/ppermute | solution.py:275
  60.6 1.7 %collective-permute-start.12 = (f32[2,32,1408]{2,1,0:T(8,128)S(1)}, f32[2,32,1408]{2,1,0:T(8,128)S(1)}, u32[]{:S(2)}, u32[]{:S(2)}) collective-permute-start(f32[2,32,1408]{2,1,0:T(8,128)S(1)} %get-tuple-element.66), channel_id=1, source_target_pairs={{0,1},{1,0},{2,3},{3,2},{4,5},{5,4},{6,7},{7,6},{8,9},{9,8},{10,11... | collective-permute-start | bytes 1081352 | tf_op jit(solution)/shard_map/ppermute | solution.py:277
  62.4 7.4 %collective-permute-start.13 = (f32[32,1408]{1,0:T(8,128)S(1)}, f32[32,1408]{1,0:T(8,128)S(1)}, u32[]{:S(2)}, u32[]{:S(2)}) collective-permute-start(f32[32,1408]{1,0:T(8,128)S(1)} %get-tuple-element.68), channel_id=1, source_target_pairs={{0,24},{4,28},{8,0},{12,4},{16,8},{20,12},{24,16},{28,20},{1,25},{... | collective-permute-start | bytes 540680 | tf_op jit(solution)/shard_map/ppermute | solution.py:275
  62.4 10.4 %collective-permute-start.14 = (f32[32,1408]{1,0:T(8,128)S(1)}, f32[32,1408]{1,0:T(8,128)S(1)}, u32[]{:S(2)}, u32[]{:S(2)}) collective-permute-start(f32[32,1408]{1,0:T(8,128)S(1)} %get-tuple-element.67), channel_id=1, source_target_pairs={{0,26},{1,27},{2,24},{3,25},{4,30},{5,31},{6,28},{7,29},{8,2},{9,3... | collective-permute-start | bytes 540680 | tf_op jit(solution)/shard_map/ppermute | solution.py:279

commit v5 on v4

--- a/solution.py
+++ b/solution.py
@@ -306,8 +306,9 @@
     powers = [sent(part, 0, 2 * d) for d, part in zip(others, powers)]
 
     keep1, give1 = correlated(w, norm, earlier, data, 0, pieces)
-    give1, got0, powers = together((give1, got0, powers))
+    give1, got0 = together((give1, got0))
     got1 = sent(give1, 0, 1)
+    got1, powers = together((got1, powers))
     num0 = [keep0[d] + got0[d] for d in others]
     num1 = [keep1[d] + got1[d] for d in range(pieces // 2)]
     earliest, _, _ = together((earliest, num0, num1))

time: 73.9 us -> 73.8 us (level)
  no operation moved by 1% of the time
where the time goes in v5:
time: 73.8 us; the launch traced here: 73.6 us
  Pallas kernels  39 us (53%)
  starting transfers between devices  20.1 us (27%)
  waiting for transfers between devices  11.7 us (16%)
  local copies, waits for them, and re-layouts  2.34 us (3%)
    pallas_call x3, Pallas kernels, correlated(): pl.pallas_call(lambda *refs: slab_kernel(open_at, *refs), in_specs=[VMEM]...  31.2 us
    ppermute x6, starting transfers between devices, sent(): lax.ppermute(block, 'tm', [(i, (i + slabs) % n) for i in range(n)])  10.1 us
    ppermute x6, waiting for transfers between devices, sent(): lax.ppermute(block, 'tm', [(i, (i + slabs) % n) for i in range(n)])  6.49 us
    ppermute x2, starting transfers between devices, sent(): return lax.ppermute(block, ('tm', 'chan'), route)  4.52 us
    ppermute x6, starting transfers between devices, sent(): return lax.ppermute(block, 'chan', [(k, k ^ distance) for k in range(m)])  3.91 us
    pallas_call x1, Pallas kernels, tap_major(): pl.pallas_call(relayout_kernel, in_specs=[VMEM] * 2, out_specs=[VMEM] * 2...  3.64 us
    ppermute x2, waiting for transfers between devices, sent(): return lax.ppermute(block, ('tm', 'chan'), route)  3.5 us
    unnamed x8, local copies, waits for them, and re-layouts  2.34 us
  transfers between devices with their start and end apart: 15, of which 4 were waited for; matrix products, arithmetic and copies ran while one was open for 0% of the time, Pallas kernels for 52%

profile of v5, /device:TPU:0, one launch (start us, length us, event | category | flops | bytes accessed | tf_op | source)
XLA Modules:
  0.0 73.6 jit_solution(9324260263895189445)
XLA Ops:
  0.0 6.0 %collective-permute-start.1 = (s32[128,256]{1,0:T(8,128)}, s32[128,256]{1,0:T(8,128)S(1)}, u32[]{:S(2)}, u32[]{:S(2)}) collective-permute-start(s32[128,256]{1,0:T(8,128)} %v0_ref.1), channel_id=1, source_target_pairs={{0,28},{4,0},{8,4},{12,8},{16,12},{20,16},{24,20},{28,24},{1,29},{... | collective-permute-start | bytes 393224 | tf_op jit(solution)/shard_map/ppermute | solution.py:275
  6.0 0.4 collective-permute-start.2
  6.4 1.1 %copy-done.2 = bf16[256,1280]{1,0:T(8,128)(2,1)S(1)} copy-done((bf16[256,1280]{1,0:T(8,128)(2,1)S(1)}, bf16[256,1280]{1,0:T(8,128)(2,1)}, u32[]{:S(2)}) %copy-start.2) | copy-done | bytes 655384
  7.6 1.6 %collective-permute-start = (bf16[256,128]{1,0:T(8,128)(2,1)S(1)}, bf16[256,128]{1,0:T(8,128)(2,1)S(1)}, u32[]{:S(2)}, u32[]{:S(2)}) collective-permute-start(bf16[256,128]{1,0:T(8,128)(2,1)S(1)} %shard_map.38), channel_id=1, source_target_pairs={{4,0},{8,4},{12,8},{16,12},{20,16},{24,20},{28,24},{5,1},{9,5},{13... | collective-permute-start | bytes 196616 | tf_op jit(solution)/shard_map/ppermute | solution.py:289
  9.1 1.2 %copy-done = bf16[128,25600]{1,0:T(8,128)(2,1)S(1)} copy-done((bf16[128,25600]{1,0:T(8,128)(2,1)S(1)}, bf16[128,25600]{1,0:T(8,128)(2,1)}, u32[]{:S(2)}) %copy-start) | copy-done | bytes 6553624
  10.4 3.6 %shard_map.37 = (bf16[103,256,128]{2,1,0:T(8,128)(2,1)S(1)}, f32[128,128]{1,0:T(8,128)S(1)}) custom-call(bf16[128,25600]{1,0:T(8,128)(2,1)S(1)} %copy-done, s32[128,256]{1,0:T(8,128)S(1)} %copy-done.1), custom_call_target="tpu_custom_call" | custom-call | bytes 13107200 | tf_op jit(solution)/shard_map/pallas_call | solution.py:177
  14.1 1.5 %collective-permute-start.4 = (bf16[256,1280]{1,0:T(8,128)(2,1)S(1)}, bf16[256,1280]{1,0:T(8,128)(2,1)S(1)}, u32[]{:S(2)}, u32[]{:S(2)}) collective-permute-start(bf16[256,1280]{1,0:T(8,128)(2,1)S(1)} %copy-done.3), channel_id=1, source_target_pairs={{0,4},{4,8},{8,12},{12,16},{16,20},{20,24},{24,28},{28,0},{1,5},{5... | collective-permute-start | bytes 1966088 | tf_op jit(solution)/shard_map/ppermute | solution.py:275
  15.6 1.5 %collective-permute-start.8 = (bf16[256,1280]{1,0:T(8,128)(2,1)S(1)}, bf16[256,1280]{1,0:T(8,128)(2,1)S(1)}, u32[]{:S(2)}, u32[]{:S(2)}) collective-permute-start(bf16[256,1280]{1,0:T(8,128)(2,1)S(1)} %copy-done.3), channel_id=1, source_target_pairs={{0,8},{4,12},{8,16},{12,20},{16,24},{20,28},{24,0},{28,4},{1,9},{5... | collective-permute-start | bytes 1966088 | tf_op jit(solution)/shard_map/ppermute | solution.py:275
  17.1 1.3 %shard_map.39 = (f32[2,3,32,1408]{3,2,1,0:T(8,128)S(1)}, f32[2,3,32,1408]{3,2,1,0:T(8,128)S(1)}) custom-call(bf16[256,1280]{1,0:T(8,128)(2,1)S(1)} %copy-done.3, bf16[256,128]{1,0:T(8,128)(2,1)S(1)} %collective-permute-done.h_ref.refs_3_, s32[128,256]{1,0:T(8,128)S(1)} %copy-done.1, s32[128,256]{1,0:T(8,128)S(1)} %collective-permute-done.1.v1_ref, ...), custom_call_target="tpu_custom_call" | custom-call | flops 503316480 | bytes 2621440 | tf_op jit(solution)/shard_map/pallas_call | solution.py:165
  18.5 10.4 %shard_map.40 = (f32[2,32,1408]{2,1,0:T(8,128)S(1)}, f32[2,32,1408]{2,1,0:T(8,128)S(1)}) custom-call(bf16[103,256,128]{2,1,0:T(8,128)(2,1)S(1)} %get-tuple-element.42.refs_0_, f32[128,128]{1,0:T(8,128)S(1)} %get-tuple-element.43.refs_1_, bf16[256,1280]{1,0:T(8,128)(2,1)S(1)} %copy-done.3, bf16[256,128]{1,0:T(8,128)(2,1)S(1)} %collective-permute-done.h_ref.refs_3_), custom_call_target="tpu_custom_call" | custom-call | flops 12582912000 | bytes 6553600 | tf_op jit(solution)/shard_map/pallas_call | solution.py:191
  28.9 1.6 %collective-permute-start.7 = (f32[3,32,1408]{2,1,0:T(8,128)S(1)}, f32[3,32,1408]{2,1,0:T(8,128)S(1)}, u32[]{:S(2)}, u32[]{:S(2)}) collective-permute-start(f32[3,32,1408]{2,1,0:T(8,128)S(1)} %add_bitcast_fusion), channel_id=1, source_target_pairs={{0,2},{1,3},{2,0},{3,1},{4,6},{5,7},{6,4},{7,5},{8,10},{9,11},{10,... | collective-permute-start | bytes 1622024 | tf_op jit(solution)/shard_map/ppermute | solution.py:277
  30.5 4.0 %collective-permute-done.4.refs_2_.refs_3_ = bf16[256,1280]{1,0:T(8,128)(2,1)S(1)} collective-permute-done((bf16[256,1280]{1,0:T(8,128)(2,1)S(1)}, bf16[256,1280]{1,0:T(8,128)(2,1)S(1)}, u32[]{:S(2)}, u32[]{:S(2)}) %collective-permute-start.4) | collective-permute-done | bytes 655392 | tf_op jit(solution)/shard_map/ppermute | solution.py:275
  34.5 10.5 %shard_map.41 = (f32[2,32,1408]{2,1,0:T(8,128)S(1)}, f32[2,32,1408]{2,1,0:T(8,128)S(1)}) custom-call(bf16[103,256,128]{2,1,0:T(8,128)(2,1)S(1)} %get-tuple-element.42.refs_0_, f32[128,128]{1,0:T(8,128)S(1)} %get-tuple-element.43.refs_1_, bf16[256,1280]{1,0:T(8,128)(2,1)S(1)} %collective-permute-done.4.refs_2_.refs_3_, bf16[256,1280]{1,0:T(8,128)(2,1)S(1)} %copy-done.3), custom_call_target="tpu_custom_call" | custom-call | flops 12582912000 | bytes 6553600 | tf_op jit(solution)/shard_map/pallas_call | solution.py:191
  45.1 0.6 collective-permute-start.6
  45.6 1.6 %collective-permute-start.11 = (f32[32,1408]{1,0:T(8,128)S(1)}, f32[32,1408]{1,0:T(8,128)S(1)}, u32[]{:S(2)}, u32[]{:S(2)}) collective-permute-start(f32[32,1408]{1,0:T(8,128)S(1)} %add_bitcast_fusion.3), channel_id=1, source_target_pairs={{0,2},{1,3},{2,0},{3,1},{4,6},{5,7},{6,4},{7,5},{8,10},{9,11},{10,... | collective-permute-start | bytes 540680 | tf_op jit(solution)/shard_map/ppermute | solution.py:277
  47.4 2.2 %collective-permute-start.10 = (f32[32,1408]{1,0:T(8,128)S(1)}, f32[32,1408]{1,0:T(8,128)S(1)}, u32[]{:S(2)}, u32[]{:S(2)}) collective-permute-start(f32[32,1408]{1,0:T(8,128)S(1)} %get-tuple-element.71), channel_id=1, source_target_pairs={{0,30},{1,31},{2,28},{3,29},{4,2},{5,3},{6,0},{7,1},{8,6},{9,7},{1... | collective-permute-start | bytes 540680 | tf_op jit(solution)/shard_map/ppermute | solution.py:279
  49.6 10.4 %shard_map.42 = (f32[2,32,1408]{2,1,0:T(8,128)S(1)}, f32[2,32,1408]{2,1,0:T(8,128)S(1)}) custom-call(bf16[103,256,128]{2,1,0:T(8,128)(2,1)S(1)} %get-tuple-element.42.refs_0_, f32[128,128]{1,0:T(8,128)S(1)} %get-tuple-element.43.refs_1_, bf16[256,1280]{1,0:T(8,128)(2,1)S(1)} %collective-permute-done.8.refs_2_, ...), custom_call_target="tpu_custom_call" | custom-call | flops 12582912000 | bytes 6553600 | tf_op jit(solution)/shard_map/pallas_call | solution.py:191
  60.1 1.7 %collective-permute-done.12 = f32[2,32,1408]{2,1,0:T(8,128)S(1)} collective-permute-done((f32[2,32,1408]{2,1,0:T(8,128)S(1)}, f32[2,32,1408]{2,1,0:T(8,128)S(1)}, u32[]{:S(2)}, u32[]{:S(2)}) %collective-permute-start.12) | collective-permute-done | bytes 360480 | tf_op jit(solution)/shard_map/ppermute | solution.py:277
  61.8 0.6 collective-permute-start.13
  62.3 2.3 %collective-permute-start.14 = (f32[32,1408]{1,0:T(8,128)S(1)}, f32[32,1408]{1,0:T(8,128)S(1)}, u32[]{:S(2)}, u32[]{:S(2)}) collective-permute-start(f32[32,1408]{1,0:T(8,128)S(1)} %get-tuple-element.69), channel_id=1, source_target_pairs={{0,26},{1,27},{2,24},{3,25},{4,30},{5,31},{6,28},{7,29},{8,2},{9,3... | collective-permute-start | bytes 540680 | tf_op jit(solution)/shard_map/ppermute | solution.py:279
  64.7 2.0 %shard_map.43 = (f32[3,32,1280]{2,1,0:T(8,128)}, f32[32,1280]{1,0:T(8,128)S(1)}, f32[32,128]{1,0:T(8,128)S(1)}) custom-call(f32[2,3,32,1408]{3,2,1,0:T(8,128)S(1)} %get-tuple-element.41.refs_0_, f32[2,3,32,1408]{3,2,1,0:T(8,128)S(1)} %collective-permute-done.3.refs_1_, f32[3,32,1408]{2,1,0:T(8,128)S(1)} %collective-permute-done.7.refs_2_, ...), custom_call_target="tpu_custom_call" | custom-call | tf_op jit(solution)/shard_map/pallas_call | solution.py:243
  66.7 2.5 %collective-permute-done.13.refs_3_ = f32[32,1408]{1,0:T(8,128)S(1)} collective-permute-done((f32[32,1408]{1,0:T(8,128)S(1)}, f32[32,1408]{1,0:T(8,128)S(1)}, u32[]{:S(2)}, u32[]{:S(2)}) %collective-permute-start.13) | collective-permute-done | bytes 180256 | tf_op jit(solution)/shard_map/ppermute | solution.py:275
  69.2 3.5 %collective-permute-done.14.refs_4_ = f32[32,1408]{1,0:T(8,128)S(1)} collective-permute-done((f32[32,1408]{1,0:T(8,128)S(1)}, f32[32,1408]{1,0:T(8,128)S(1)}, u32[]{:S(2)}, u32[]{:S(2)}) %collective-permute-start.14) | collective-permute-done | bytes 180256 | tf_op jit(solution)/shard_map/ppermute | solution.py:279
  72.7 0.8 %shard_map.44 = f32[3,32,1280]{2,1,0:T(8,128)} custom-call(f32[3,32,1280]{2,1,0:T(8,128)} %get-tuple-element.64.refs_0_, f32[32,1280]{1,0:T(8,128)S(1)} %get-tuple-element.65.refs_1_, f32[32,128]{1,0:T(8,128)S(1)} %get-tuple-element.66.refs_2_, f32[32,1408]{1,0:T(8,128)S(1)} %collective-permute-done.13.refs_3_, ...), custom_call_target="tpu_custom_call", output_to_operand_aliasing={{}: (0, {})} | custom-call | tf_op jit(solution)/shard_map/pallas_call | solution.py:261
  (26 shorter events, 0.4 us)
Async XLA Ops:
  0.0 9.1 %copy-start.1 = (s32[128,256]{1,0:T(8,128)S(1)}, s32[128,256]{1,0:T(8,128)}, u32[]{:S(2)}) copy-start(s32[128,256]{1,0:T(8,128)} %v0_ref.1) | copy-start | bytes 393220
  0.0 14.0 %collective-permute-start.1 = (s32[128,256]{1,0:T(8,128)}, s32[128,256]{1,0:T(8,128)S(1)}, u32[]{:S(2)}, u32[]{:S(2)}) collective-permute-start(s32[128,256]{1,0:T(8,128)} %v0_ref.1), channel_id=1, source_target_pairs={{0,28},{4,0},{8,4},{12,8},{16,12},{20,16},{24,20},{28,24},{1,29},{... | collective-permute-start | bytes 393224 | tf_op jit(solution)/shard_map/ppermute | solution.py:275
  6.0 8.1 %collective-permute-start.2 = (s32[128,256]{1,0:T(8,128)}, s32[128,256]{1,0:T(8,128)S(1)}, u32[]{:S(2)}, u32[]{:S(2)}) collective-permute-start(s32[128,256]{1,0:T(8,128)} %v0_ref.1), channel_id=1, source_target_pairs={{0,24},{4,28},{8,0},{12,4},{16,8},{20,12},{24,16},{28,20},{1,25},{... | collective-permute-start | bytes 393224 | tf_op jit(solution)/shard_map/ppermute | solution.py:275
  6.4 1.1 %copy-start.2 = (bf16[256,1280]{1,0:T(8,128)(2,1)S(1)}, bf16[256,1280]{1,0:T(8,128)(2,1)}, u32[]{:S(2)}) copy-start(bf16[256,1280]{1,0:T(8,128)(2,1)} %refs_3_.1) | copy-start | bytes 1966084
  7.5 2.9 %copy-start = (bf16[128,25600]{1,0:T(8,128)(2,1)S(1)}, bf16[128,25600]{1,0:T(8,128)(2,1)}, u32[]{:S(2)}) copy-start(bf16[128,25600]{1,0:T(8,128)(2,1)} %t_ref.1) | copy-start | bytes 19660804
  7.5 6.5 %copy-start.3 = (bf16[256,1280]{1,0:T(8,128)(2,1)S(1)}, bf16[256,1280]{1,0:T(8,128)(2,1)}, u32[]{:S(2)}) copy-start(bf16[256,1280]{1,0:T(8,128)(2,1)} %refs_3_.1) | copy-start | bytes 1966084
  7.6 6.5 %collective-permute-start = (bf16[256,128]{1,0:T(8,128)(2,1)S(1)}, bf16[256,128]{1,0:T(8,128)(2,1)S(1)}, u32[]{:S(2)}, u32[]{:S(2)}) collective-permute-start(bf16[256,128]{1,0:T(8,128)(2,1)S(1)} %shard_map.38), channel_id=1, source_target_pairs={{4,0},{8,4},{12,8},{16,12},{20,16},{24,20},{28,24},{5,1},{9,5},{13... | collective-permute-start | bytes 196616 | tf_op jit(solution)/shard_map/ppermute | solution.py:289
  14.1 20.4 %collective-permute-start.4 = (bf16[256,1280]{1,0:T(8,128)(2,1)S(1)}, bf16[256,1280]{1,0:T(8,128)(2,1)S(1)}, u32[]{:S(2)}, u32[]{:S(2)}) collective-permute-start(bf16[256,1280]{1,0:T(8,128)(2,1)S(1)} %copy-done.3), channel_id=1, source_target_pairs={{0,4},{4,8},{8,12},{12,16},{16,20},{20,24},{24,28},{28,0},{1,5},{5... | collective-permute-start | bytes 1966088 | tf_op jit(solution)/shard_map/ppermute | solution.py:275
  15.6 34.0 %collective-permute-start.8 = (bf16[256,1280]{1,0:T(8,128)(2,1)S(1)}, bf16[256,1280]{1,0:T(8,128)(2,1)S(1)}, u32[]{:S(2)}, u32[]{:S(2)}) collective-permute-start(bf16[256,1280]{1,0:T(8,128)(2,1)S(1)} %copy-done.3), channel_id=1, source_target_pairs={{0,8},{4,12},{8,16},{12,20},{16,24},{20,28},{24,0},{28,4},{1,9},{5... | collective-permute-start | bytes 1966088 | tf_op jit(solution)/shard_map/ppermute | solution.py:275
  18.4 10.4 %collective-permute-start.3 = (f32[2,3,32,1408]{3,2,1,0:T(8,128)S(1)}, f32[2,3,32,1408]{3,2,1,0:T(8,128)S(1)}, u32[]{:S(2)}, u32[]{:S(2)}) collective-permute-start(f32[2,3,32,1408]{3,2,1,0:T(8,128)S(1)} %get-tuple-element.47), channel_id=1, source_target_pairs={{0,1},{1,0},{2,3},{3,2},{4,5},{5,4},{6,7},{7,6},{8,9},{9,8},{10,11... | collective-permute-start | bytes 3244040 | tf_op jit(solution)/shard_map/ppermute | solution.py:277
  28.9 18.3 %collective-permute-start.7 = (f32[3,32,1408]{2,1,0:T(8,128)S(1)}, f32[3,32,1408]{2,1,0:T(8,128)S(1)}, u32[]{:S(2)}, u32[]{:S(2)}) collective-permute-start(f32[3,32,1408]{2,1,0:T(8,128)S(1)} %add_bitcast_fusion), channel_id=1, source_target_pairs={{0,2},{1,3},{2,0},{3,1},{4,6},{5,7},{6,4},{7,5},{8,10},{9,11},{10,... | collective-permute-start | bytes 1622024 | tf_op jit(solution)/shard_map/ppermute | solution.py:277
  34.5 10.5 %collective-permute-start.5 = (f32[2,32,1408]{2,1,0:T(8,128)S(1)}, f32[2,32,1408]{2,1,0:T(8,128)S(1)}, u32[]{:S(2)}, u32[]{:S(2)}) collective-permute-start(f32[2,32,1408]{2,1,0:T(8,128)S(1)} %get-tuple-element.52), channel_id=1, source_target_pairs={{0,1},{1,0},{2,3},{3,2},{4,5},{5,4},{6,7},{7,6},{8,9},{9,8},{10,11... | collective-permute-start | bytes 1081352 | tf_op jit(solution)/shard_map/ppermute | solution.py:277
  45.1 2.2 %collective-permute-start.6 = (f32[2,32,1408]{2,1,0:T(8,128)S(1)}, f32[2,32,1408]{2,1,0:T(8,128)S(1)}, u32[]{:S(2)}, u32[]{:S(2)}) collective-permute-start(f32[2,32,1408]{2,1,0:T(8,128)S(1)} %get-tuple-element.53), channel_id=1, source_target_pairs={{0,1},{1,0},{2,3},{3,2},{4,5},{5,4},{6,7},{7,6},{8,9},{9,8},{10,11... | collective-permute-start | bytes 1081352 | tf_op jit(solution)/shard_map/ppermute | solution.py:277
  45.6 14.3 %collective-permute-start.11 = (f32[32,1408]{1,0:T(8,128)S(1)}, f32[32,1408]{1,0:T(8,128)S(1)}, u32[]{:S(2)}, u32[]{:S(2)}) collective-permute-start(f32[32,1408]{1,0:T(8,128)S(1)} %add_bitcast_fusion.3), channel_id=1, source_target_pairs={{0,2},{1,3},{2,0},{3,1},{4,6},{5,7},{6,4},{7,5},{8,10},{9,11},{10,... | collective-permute-start | bytes 540680 | tf_op jit(solution)/shard_map/ppermute | solution.py:277
  47.3 12.7 %collective-permute-start.9 = (f32[32,1408]{1,0:T(8,128)S(1)}, f32[32,1408]{1,0:T(8,128)S(1)}, u32[]{:S(2)}, u32[]{:S(2)}) collective-permute-start(f32[32,1408]{1,0:T(8,128)S(1)} %get-tuple-element.72), channel_id=1, source_target_pairs={{0,28},{4,0},{8,4},{12,8},{16,12},{20,16},{24,20},{28,24},{1,29},{... | collective-permute-start | bytes 540680 | tf_op jit(solution)/shard_map/ppermute | solution.py:275
  47.4 12.6 %collective-permute-start.10 = (f32[32,1408]{1,0:T(8,128)S(1)}, f32[32,1408]{1,0:T(8,128)S(1)}, u32[]{:S(2)}, u32[]{:S(2)}) collective-permute-start(f32[32,1408]{1,0:T(8,128)S(1)} %get-tuple-element.71), channel_id=1, source_target_pairs={{0,30},{1,31},{2,28},{3,29},{4,2},{5,3},{6,0},{7,1},{8,6},{9,7},{1... | collective-permute-start | bytes 540680 | tf_op jit(solution)/shard_map/ppermute | solution.py:279
  60.0 1.7 %collective-permute-start.12 = (f32[2,32,1408]{2,1,0:T(8,128)S(1)}, f32[2,32,1408]{2,1,0:T(8,128)S(1)}, u32[]{:S(2)}, u32[]{:S(2)}) collective-permute-start(f32[2,32,1408]{2,1,0:T(8,128)S(1)} %get-tuple-element.68), channel_id=1, source_target_pairs={{0,1},{1,0},{2,3},{3,2},{4,5},{5,4},{6,7},{7,6},{8,9},{9,8},{10,11... | collective-permute-start | bytes 1081352 | tf_op jit(solution)/shard_map/ppermute | solution.py:277
  61.8 7.4 %collective-permute-start.13 = (f32[32,1408]{1,0:T(8,128)S(1)}, f32[32,1408]{1,0:T(8,128)S(1)}, u32[]{:S(2)}, u32[]{:S(2)}) collective-permute-start(f32[32,1408]{1,0:T(8,128)S(1)} %get-tuple-element.70), channel_id=1, source_target_pairs={{0,24},{4,28},{8,0},{12,4},{16,8},{20,12},{24,16},{28,20},{1,25},{... | collective-permute-start | bytes 540680 | tf_op jit(solution)/shard_map/ppermute | solution.py:275
  62.3 10.4 %collective-permute-start.14 = (f32[32,1408]{1,0:T(8,128)S(1)}, f32[32,1408]{1,0:T(8,128)S(1)}, u32[]{:S(2)}, u32[]{:S(2)}) collective-permute-start(f32[32,1408]{1,0:T(8,128)S(1)} %get-tuple-element.69), channel_id=1, source_target_pairs={{0,26},{1,27},{2,24},{3,25},{4,30},{5,31},{6,28},{7,29},{8,2},{9,3... | collective-permute-start | bytes 540680 | tf_op jit(solution)/shard_map/ppermute | solution.py:279
